TPU v7x, 256 devices: a whole 4x4x8 slice. The times are simulated.
256 devices in a mesh: lon: 32 (over z, x_hi, core), lat: 8 (over y, x_lo).
Axes of the slice: x: 4 (x_hi: 2, x_lo: 2; x = x_hi * 2 + x_lo), y: 4, z: 8, core: 2. Of those that a mesh axis runs over, the one named last changes fastest.
Arguments:
- increment: float32 [512, 512, 256], P('lat', 'lon'), may hold values from -8 to 8
- error_std: float32 [512, 512, 256], P('lat', 'lon'), may hold values from 0.3 to 3
- vertical: float32 [4, 64, 64], replicated, may hold values from -0.75 to 0.75
- lon_decay: float32 [512, 256], P('lon'), may hold values from 0 to 1, as said below
- lat_decay: float32 [512, 256], P('lat'), may hold values from 0 to 1, as said below
Outputs:
- result_field: float32 [512, 512, 256], P('lat', 'lon')
Inputs may be any that keep to these rules, and one draw needn't show every extreme that they name: `lon_decay`: every entry is positive and below 1 - 0.07 / 512. `lat_decay`: every entry is positive and below 1.
All inputs are finite; a program needn't handle non-finite values.
Results may differ from a plain program's by a relative error of at most 0.0003.
Values sent between devices are 32-bit elements; how exact they have to be, the bound alone decides.
A program may use at most 128 MiB of HBM per device.

v0:
```python
import jax
import jax.numpy as jnp
from jax import lax
from jax.sharding import PartitionSpec as P

PRECISE = lax.Precision.HIGHEST


def entering_2(array, axis, combine, identity, reverse):
    peers, index = (lax.axis_size(axis), lax.axis_index(axis))
    everything = jax.tree.map(lambda part: lax.all_gather(part, axis), array)
    start = jax.tree.map(
        lambda part, zero: jnp.broadcast_to(jnp.asarray(zero, part.dtype), part.shape),
        array,
        identity,
    )

    def step(k, before):
        at = peers - 1 - k if reverse else k
        reached = at > index if reverse else at < index
        new = combine(before, jax.tree.map(lambda part: part[at], everything))
        return jax.tree.map(lambda a, b: jnp.where(reached, a, b), new, before)

    return lax.fori_loop(0, peers, step, start)


def spread(array, axis, root):
    mine = lax.axis_index(axis) == root
    return lax.psum(jnp.where(mine, array, jnp.zeros_like(array)), axis)


def block_matrix(vertical):
    var_count = vertical.shape[0]
    lev_count = vertical.shape[1]
    selector = jnp.eye(var_count, dtype=vertical.dtype)
    expanded = vertical[:, :, None, :] * selector[:, None, :, None]
    return expanded.reshape(var_count * lev_count, var_count * lev_count)


def local_sweep(values, decays):
    length = values.shape[0]
    log_sums = jnp.cumsum(jnp.log(decays), axis=0)
    lower_mask = (jnp.arange(length)[:, None] >= jnp.arange(length)[None, :])[:, :, None]
    exponent = jnp.where(lower_mask, log_sums[:, None, :] - log_sums[None, :, :], 0.0)
    kernel = jnp.where(lower_mask, jnp.exp(exponent), 0.0) * (1.0 - decays)[None, :, :]
    starting_blank = jnp.einsum("ijc,jrc->irc", kernel, values, precision=PRECISE)
    return (starting_blank, jnp.exp(log_sums))


def compose(earlier, later):
    return (earlier[0] * later[0], later[0][..., None, :] * earlier[1] + later[1])


def lon_sweep(values, decays, backward):
    if backward:
        values, decays = (values[::-1], decays[::-1])
    starting_blank, growth = local_sweep(values, decays)
    own_map = (growth[-1], starting_blank[-1])
    identity = (jnp.ones_like(own_map[0]), jnp.zeros_like(own_map[1]))
    incoming = entering_2(own_map, "lon", compose, identity, backward)
    root_index = 0 if backward else lax.axis_size("lon") - 1
    loop_map = jax.tree.map(
        lambda part: spread(part, "lon", root_index), compose(incoming, own_map)
    )
    loop_state = loop_map[1] / (1.0 - loop_map[0])[None, :]
    entering = incoming[0][None, :] * loop_state + incoming[1]
    swept_line = starting_blank + growth[:, None, :] * entering[None]
    if backward:
        swept_line = swept_line[::-1]
    return swept_line


def lat_sweep(values, decays, backward):
    if backward:
        values, decays = (values[::-1], decays[::-1])
    starting_blank, growth = local_sweep(values, decays)
    own_map = (growth[-1], starting_blank[-1])
    identity = (jnp.ones_like(own_map[0]), jnp.zeros_like(own_map[1]))
    incoming = entering_2(own_map, "lat", compose, identity, backward)
    swept_line = starting_blank + growth[:, None, :] * incoming[1][None]
    if backward:
        swept_line = swept_line[::-1]
    return swept_line


def per_device(increment, error_std, vertical, lon_decay, lat_decay):
    vert_block = block_matrix(vertical)
    working = jnp.einsum("abk,kl->abl", error_std * increment, vert_block, precision=PRECISE)
    column_list = jnp.swapaxes(working, 0, 1)
    for repeat in range(2):
        column_list = lon_sweep(column_list, lon_decay, False)
        column_list = lon_sweep(column_list, lon_decay, True)
    working = jnp.swapaxes(column_list, 0, 1)
    for repeat in range(2):
        working = lat_sweep(working, lat_decay, False)
        working = lat_sweep(working, lat_decay, True)
    return error_std * jnp.einsum("abl,kl->abk", working, vert_block, precision=PRECISE)


def solution(mesh):
    placed = (P("lat", "lon", None), P("lat", "lon", None), P(), P("lon", None), P("lat", None))
    return jax.shard_map(
        per_device, mesh=mesh, in_specs=placed, out_specs=P("lat", "lon", None), check_vma=False
    )
```

profile of v0, /device:TPU:2, one launch (start us, length us, event | category | flops | bytes accessed | tf_op | source)
XLA Modules:
  0.0 1725.0 jit_solution(13349470813158219444)
XLA Ops:
  19.3 43.8 %all-gather = f32[32,1,256]{2,1,0:T(1,128)S(1)} all-gather(f32[1,1,256]{2,1,0:T(1,128)S(1)} %get-tuple-element.1296), channel_id=1, replica_groups=mesh['lon'=32,'lat'=8] {'lon'}, dimensions={0}, use_global_device_ids=true | all-gather | bytes 33792 | tf_op jit(solution)/shard_map/all_gather | solution.py:11
  63.4 37.9 %all-gather.9.cloned.1.call-done = f32[32,64,256]{2,1,0:T(8,128)} async-done(((f32[1,64,256]{2,1,0:T(8,128)}), f32[32,64,256]{2,1,0:T(8,128)}) %all-gather.9.cloned.1.call-update) | async-done | bytes 2097168 | tf_op jit(solution)/shard_map/all_gather | solution.py:11
  101.2 29.4 %while.128 = (s32[]{:T(128)}, f32[256]{0:T(256)S(1)}, f32[64,256]{1,0:T(8,128)S(1)}, s32[]{:T(128)}, f32[32,256]{1,0:T(8,128)S(1)}, /*index=5*/f32[32,64,256]{2,1,0:T(8,128)}, s32[]{:T(128)}, s32[]{:T(128)}) while((s32[]{:T(128)}, f32[256]{0:T(256)S(1)}, f32[64,256]{1,0:T(8,128)S(1)}, s32[]{:T(128)}, f32[32,256]{1,0:T(8,128)S(1)}, ...), condition=%wide.region_2.3_spmd.clone, body=%wide.region_1.2_spmd.clone.sunk | while | flops 66308 | bytes 202867 | solution.py:24
  131.6 67.6 %psum.57 = f32[256]{0:T(256)S(1)} all-reduce(f32[256]{0:T(256)S(1)} %multiply_select_fusion.7), channel_id=1, replica_groups=mesh['lon'=32,'lat'=8] {'lon'}, use_global_device_ids=true, to_apply=%region_4.5 | all-reduce | flops 256 | bytes 2048 | tf_op jit(solution)/shard_map/psum | solution.py:29
  199.2 175.2 %all-reduce.5.cloned.1.call-done = f32[64,256]{0,1:T(8,128)} async-done(((f32[64,256]{0,1:T(8,128)}), f32[64,256]{0,1:T(8,128)}) %all-reduce.5.cloned.1.call-update) | async-done | bytes 65552 | tf_op jit(solution)/shard_map/psum | solution.py:29
  387.9 36.4 %all-gather.1 = f32[32,1,256]{2,1,0:T(1,128)S(1)} all-gather(f32[1,1,256]{2,1,0:T(1,128)S(1)} %get-tuple-element.1292), channel_id=1, replica_groups=mesh['lon'=32,'lat'=8] {'lon'}, dimensions={0}, use_global_device_ids=true | all-gather | bytes 33792 | tf_op jit(solution)/shard_map/all_gather | solution.py:11
  424.3 41.6 %all-gather.11.cloned.1.call-done = f32[32,64,256]{2,1,0:T(8,128)} async-done(((f32[1,64,256]{2,1,0:T(8,128)}), f32[32,64,256]{2,1,0:T(8,128)}) %all-gather.11.cloned.1.call-update) | async-done | bytes 2097168 | tf_op jit(solution)/shard_map/all_gather | solution.py:11
  466.0 29.8 %while.129 = (s32[]{:T(128)}, f32[256]{0:T(256)S(1)}, f32[64,256]{1,0:T(8,128)S(1)}, s32[]{:T(128)}, f32[32,256]{1,0:T(8,128)S(1)}, /*index=5*/f32[32,64,256]{2,...) while((s32[]{:T(128)}, f32[256]{0:T(256)S(1)}, f32[64,256]{1,0:T(8,128)S(1)}, s32[]{:T(128)}, ...), condition=%wide.region_7.8_spmd.clone, body=%wide.region_6.7_spmd.clone.sunk | while | flops 66312 | bytes 202929 | solution.py:24
  498.2 67.8 %psum.59 = f32[256]{0:T(256)S(1)} all-reduce(f32[256]{0:T(256)S(1)} %multiply_select_fusion.6), channel_id=1, replica_groups=mesh['lon'=32,'lat'=8] {'lon'}, use_global_device_ids=true, to_apply=%region_9.10 | all-reduce | flops 256 | bytes 2048 | tf_op jit(solution)/shard_map/psum | solution.py:29
  566.0 175.0 %all-reduce.7.cloned.1.call-done = f32[64,256]{0,1:T(8,128)} async-done(((f32[64,256]{0,1:T(8,128)}), f32[64,256]{0,1:T(8,128)}) %all-reduce.7.cloned.1.call-update) | async-done | bytes 65552 | tf_op jit(solution)/shard_map/psum | solution.py:29
  751.3 78.1 %all-gather.13.cloned.1.call-done = f32[32,64,256]{2,1,0:T(8,128)} async-done(((f32[1,64,256]{2,1,0:T(8,128)}), f32[32,64,256]{2,1,0:T(8,128)}) %all-gather.13.cloned.1.call-update) | async-done | bytes 2097168 | tf_op jit(solution)/shard_map/all_gather | solution.py:11
  829.4 29.4 %while.130 = (s32[]{:T(128)}, f32[256]{0:T(256)S(1)}, f32[64,256]{1,0:T(8,128)S(1)}, s32[]{:T(128)}, f32[32,256]{1,0:T(8,128)S(1)}, /*index=5*/f32[32,64,256]{2,1,0:T(8,128)}, s32[]{:T(128)}, s32[]{:T(128)}) while((s32[]{:T(128)}, f32[256]{0:T(256)S(1)}, f32[64,256]{1,0:T(8,128)S(1)}, s32[]{:T(128)}, f32[32,256]{1,0:T(8,128)S(1)}, ...), condition=%wide.region_11.12_spmd.clone, body=%wide.region_10.11_spmd.clone.sunk | while | flops 66308 | bytes 202867 | solution.py:24
  859.8 67.6 %psum.61 = f32[256]{0:T(256)S(1)} all-reduce(f32[256]{0:T(256)S(1)} %multiply_select_fusion.5), channel_id=1, replica_groups=mesh['lon'=32,'lat'=8] {'lon'}, use_global_device_ids=true, to_apply=%region_13.14 | all-reduce | flops 256 | bytes 2048 | tf_op jit(solution)/shard_map/psum | solution.py:29
  927.4 175.2 %all-reduce.9.cloned.1.call-done = f32[64,256]{0,1:T(8,128)} async-done(((f32[64,256]{0,1:T(8,128)}), f32[64,256]{0,1:T(8,128)}) %all-reduce.9.cloned.1.call-update) | async-done | bytes 65552 | tf_op jit(solution)/shard_map/psum | solution.py:29
  1132.1 18.5 %all-gather.3 = f32[8,1,256]{2,1,0:T(1,128)S(1)} all-gather(f32[1,1,256]{2,1,0:T(1,128)S(1)} %slice_bitcast_fusion), channel_id=1, replica_groups=mesh['lon'=32,'lat'=8] {'lat'}, dimensions={0}, use_global_device_ids=true | all-gather | bytes 9216 | tf_op jit(solution)/shard_map/all_gather | solution.py:11
  1150.6 42.0 %all-gather.15.cloned.1.call-done = f32[32,64,256]{2,1,0:T(8,128)} async-done(((f32[1,64,256]{2,1,0:T(8,128)}), f32[32,64,256]{2,1,0:T(8,128)}) %all-gather.15.cloned.1.call-update) | async-done | bytes 2097168 | tf_op jit(solution)/shard_map/all_gather | solution.py:11
  1192.6 51.3 %while.131 = (s32[]{:T(128)}, f32[256]{0:T(256)S(1)}, f32[64,256]{1,0:T(8,128)S(1)}, s32[]{:T(128)}, f32[32,256]{1,0:T(8,128)}, /*index=5*/f32[32,64,256]{2,1,0:...) while((s32[]{:T(128)}, f32[256]{0:T(256)S(1)}, f32[64,256]{1,0:T(8,128)S(1)}, s32[]{:T(128)}, ...), condition=%wide.region_15.16_spmd.clone, body=%wide.region_14.15_spmd.clone.sunk | while | flops 66312 | bytes 202929 | solution.py:24
  1245.7 67.6 %psum.63 = f32[256]{0:T(256)S(1)} all-reduce(f32[256]{0:T(256)S(1)} %multiply_select_fusion.4), channel_id=1, replica_groups=mesh['lon'=32,'lat'=8] {'lon'}, use_global_device_ids=true, to_apply=%region_17.18 | all-reduce | flops 256 | bytes 2048 | tf_op jit(solution)/shard_map/psum | solution.py:29
  1313.3 175.2 %all-reduce.11.cloned.1.call-done = f32[64,256]{0,1:T(8,128)} async-done(((f32[64,256]{0,1:T(8,128)}), f32[64,256]{0,1:T(8,128)}) %all-reduce.11.cloned.1.call-update) | async-done | bytes 65552 | tf_op jit(solution)/shard_map/psum | solution.py:29
  1494.9 16.2 fusion.38
  1515.6 28.4 %all_gather.47 = f32[8,16,256]{2,1,0:T(8,128)S(1)} all-gather(f32[1,16,256]{2,1,0:T(8,128)S(1)} %copy.75), channel_id=1, replica_groups=mesh['lon'=32,'lat'=8] {'lat'}, dimensions={0}, use_global_device_ids=true | all-gather | bytes 147456 | tf_op jit(solution)/shard_map/all_gather | solution.py:11
  1570.5 28.3 %all_gather.49 = f32[8,16,256]{2,1,0:T(8,128)S(1)} all-gather(f32[1,16,256]{2,1,0:T(8,128)S(1)} %copy.81), channel_id=1, replica_groups=mesh['lon'=32,'lat'=8] {'lat'}, dimensions={0}, use_global_device_ids=true | all-gather | bytes 147456 | tf_op jit(solution)/shard_map/all_gather | solution.py:11
  1625.2 28.3 %all_gather.50 = f32[8,16,256]{2,1,0:T(8,128)S(1)} all-gather(f32[1,16,256]{2,1,0:T(8,128)S(1)} %copy.83), channel_id=1, replica_groups=mesh['lon'=32,'lat'=8] {'lat'}, dimensions={0}, use_global_device_ids=true | all-gather | bytes 147456 | tf_op jit(solution)/shard_map/all_gather | solution.py:11
  1679.9 28.3 %all_gather.51 = f32[8,16,256]{2,1,0:T(8,128)S(1)} all-gather(f32[1,16,256]{2,1,0:T(8,128)S(1)} %copy.85), channel_id=1, replica_groups=mesh['lon'=32,'lat'=8] {'lat'}, dimensions={0}, use_global_device_ids=true | all-gather | bytes 147456 | tf_op jit(solution)/shard_map/all_gather | solution.py:11
  (604 shorter events, 308.1 us)
Async XLA Ops:
  6.5 2.5 copy-start
  6.5 94.7 %all-gather.9.cloned.1.call-start = ((), (), s32[]{:S(2)}) async-start(), calls=%async_computation | async-start | bytes 2162688 | tf_op jit(solution)/shard_map/all_gather | solution.py:11
  14.0 5.1 copy-start.6
  19.0 355.3 %all-reduce.5.cloned.1.call-start = ((), (), s32[]{:S(2)}) async-start(), calls=%async_computation.1 | async-start | bytes 262144 | tf_op jit(solution)/shard_map/psum | solution.py:29
  131.5 334.5 %all-gather.11.cloned.1.call-start = ((), (), s32[]{:S(2)}) async-start(), calls=%async_computation.2 | async-start | bytes 2162688 | tf_op jit(solution)/shard_map/all_gather | solution.py:11
  385.7 1.3 copy-start.2
  387.8 353.2 %all-reduce.7.cloned.1.call-start = ((), (), s32[]{:S(2)}) async-start(), calls=%async_computation.3 | async-start | bytes 262144 | tf_op jit(solution)/shard_map/psum | solution.py:29
  495.8 0.6 copy-start.7
  498.2 331.3 %all-gather.13.cloned.1.call-start = ((), (), s32[]{:S(2)}) async-start(), calls=%async_computation.4 | async-start | bytes 2162688 | tf_op jit(solution)/shard_map/all_gather | solution.py:11
  749.1 1.3 copy-start.3
  751.3 351.3 %all-reduce.9.cloned.1.call-start = ((), (), s32[]{:S(2)}) async-start(), calls=%async_computation.5 | async-start | bytes 262144 | tf_op jit(solution)/shard_map/psum | solution.py:29
  859.7 332.9 %all-gather.15.cloned.1.call-start = ((), (), s32[]{:S(2)}) async-start(), calls=%async_computation.6 | async-start | bytes 2162688 | tf_op jit(solution)/shard_map/all_gather | solution.py:11
  1111.7 2.8 copy-start.4
  1112.3 1.3 copy-start.1
  1114.4 374.2 %all-reduce.11.cloned.1.call-start = ((), (), s32[]{:S(2)}) async-start(), calls=%async_computation.7 | async-start | bytes 262144 | tf_op jit(solution)/shard_map/psum | solution.py:29
  1491.8 3.2 copy-start.5
Sparse Core Ops, SparseCore 0:
  19.1 82.0 all-gather.8
  131.6 242.6 all-reduce.4
  387.9 78.0 all-gather.10
  498.3 242.6 all-reduce.6
  751.4 77.9 all-gather.12
  859.8 242.6 all-reduce.8
  1114.5 78.0 all-gather.14
  1245.8 242.6 all-reduce.10
where the time goes:
time: 1740 us; the launch traced here: 1720 us
  waiting for transfers between devices  900 us (52%)
  blocking collectives  499 us (29%)
  other arithmetic  138 us (8%)
  local copies, waits for them, and re-layouts  84.4 us (5%)
  matrix products  83.5 us (5%)
    psum x4, waiting for transfers between devices, spread(): return lax.psum(jnp.where(mine, array, jnp.zeros_like(array)), axis)  701 us
    psum x4, blocking collectives, spread(): return lax.psum(jnp.where(mine, array, jnp.zeros_like(array)), axis)  271 us
    all_gather x8, blocking collectives, entering_2(): everything = jax.tree.map(lambda part: lax.all_gather(part, axis), array)  228 us
    all_gather x4, waiting for transfers between devices, entering_2(): everything = jax.tree.map(lambda part: lax.all_gather(part, axis), array)  200 us
    select_n x288, other arithmetic, step(): return jax.tree.map(lambda a, b: jnp.where(reached, a, b), new, before)  113 us
    dot_general x8, matrix products, local_sweep(): jnp.einsum('ijc,jrc->irc', kernel, values, precision=PRECISE)  78.1 us
  transfers between devices with their start and end apart: 8, of which 8 were waited for; matrix products, arithmetic and copies ran while one was open for 0% of the time, Pallas kernels for 0%

commit v1 on v0

v1 whole, which is shorter than its diff:
```python
import jax
import jax.numpy as jnp
from jax import lax
from jax.experimental import pallas as pl
from jax.experimental.pallas import tpu as pltpu
from jax.sharding import PartitionSpec as P

MESH = pl.DeviceIdType.MESH
F32 = jnp.float32
BF16 = jnp.bfloat16
NLAT, NLON, LANES = 64, 16, 128
ROWS = NLAT * NLON
CHIPS, LATS = 16, 8
HALF = range(2)
STATES = range(4)


def split(x):
    high = x.astype(BF16)
    return high, (x - high.astype(F32)).astype(BF16)


def dot3(x, high_ref, low_ref):
    high, low = split(x)
    dot = lambda a, b: jnp.dot(a, b, preferred_element_type=F32)
    return dot(high, high_ref[...]) + (dot(low, high_ref[...]) + dot(high, low_ref[...]))


def one_hot(k):
    return jnp.where(lax.broadcasted_iota(jnp.int32, (8, LANES), 0) == k, 1.0, 0.0).astype(F32)


def store_coefs(ref, at, base, ends):
    e1, e2, e3, e4 = ends
    for row, part in enumerate((e1[0:1], e2[0:1], e3[1:2], e3[0:1], e4[1:2], e4[0:1])):
        ref[(*at, pl.ds(base + row, 1), slice(None))] = part
    ref[(*at, pl.ds(base + 6, 2), slice(None))] = jnp.zeros((2, LANES), F32)


def kernel(
    inc, std, vert, lond, latd, out,
    inc_v, std_v, vert_v, lond_v, latd_v, out_v,
    vhi, vlo, thi, tlo, work, temp, lonu, latu, adj, xcol,
    pair_out, seg, segco, chipco, coin,
    s_out, s_in, x_out, x_in, unm, xlon,
    latz, latc, latx, latcx,
    lsem, osem, ssem, rsem,
):
    lon, lat = lax.axis_index("lon"), lax.axis_index("lat")
    core, chip = lax.rem(lon, 2), lon // 2
    other = 1 - core
    partner = {"lon": 2 * chip + other}
    chip_at = lambda k: lax.rem(chip + k, CHIPS)
    peer = lambda k: {"lon": 2 * chip_at(k) + core}
    lat_peer = lambda k: {"lat": lax.rem(lat + k, LATS)}

    barrier = pltpu.get_barrier_semaphore()
    pl.semaphore_signal(barrier, inc=1, device_id=partner, device_id_type=MESH)
    for k in range(1, CHIPS):
        pl.semaphore_signal(barrier, inc=1, device_id=peer(k), device_id_type=MESH)
    for k in range(1, LATS):
        pl.semaphore_signal(barrier, inc=1, device_id=lat_peer(k), device_id_type=MESH)

    loads = [pltpu.make_async_copy(a, b, lsem.at[i]) for i, (a, b) in enumerate(((lond, lond_v), (vert, vert_v), (latd, latd_v)))]
    for copy in loads:
        copy.start()
    parts = 4
    size = ROWS // parts
    big = []
    for i in range(parts):
        rows = pl.ds(i * size, size)
        big.append((
            pltpu.make_async_copy(inc.at[rows], inc_v.at[rows], lsem.at[3 + 2 * i]),
            pltpu.make_async_copy(std.at[rows], std_v.at[rows], lsem.at[4 + 2 * i]),
        ))
        for copy in big[-1]:
            copy.start()

    def send(src, dst, which, device):
        copy = pltpu.make_async_remote_copy(
            src_ref=src, dst_ref=dst, send_sem=ssem.at[which], recv_sem=rsem.at[which],
            device_id=device, device_id_type=MESH,
        )
        copy.start()

    def arrived(ref, which):
        pltpu.make_async_copy(ref, ref, rsem.at[which]).wait()

    def sent(ref, which):
        pltpu.make_async_copy(ref, ref, ssem.at[which]).wait()

    loads[0].wait()
    lanes = lambda h: pl.ds(h * LANES, LANES)
    lon_row = lambda i, h: lond_v[pl.ds(i, 1), lanes(h)]
    for h in HALF:
        ends = []
        line = [None] * NLON
        for k in STATES:
            y = one_hot(k)
            for i in range(NLON) if k % 2 == 0 else reversed(range(NLON)):
                d = lon_row(i, h)
                y = d * y if line[i] is None else d * y + (1.0 - d) * line[i]
                line[i] = y
            ends.append(y)
        for i in range(NLON):
            lonu[h, pl.ds(8 * i, 8), :] = line[i]
        store_coefs(segco, (core, h), 0, ends)

    loads[1].wait()
    vhi[...] = jnp.zeros_like(vhi)
    vlo[...] = jnp.zeros_like(vlo)
    thi[...] = jnp.zeros_like(thi)
    tlo[...] = jnp.zeros_like(tlo)
    zero64 = jnp.zeros((64, 64), F32)
    for p in range(2):
        a, b = vert_v[2 * p], vert_v[2 * p + 1]
        block = jnp.concatenate(
            [jnp.concatenate([a, zero64], axis=1), jnp.concatenate([zero64, b], axis=1)], axis=0
        )
        at = (pl.ds(p * LANES, LANES), pl.ds(p * LANES, LANES))
        vhi[at], vlo[at] = split(block)
        thi[at], tlo[at] = split(block.T)

    for i in range(parts):
        for copy in big[i]:
            copy.wait()
        rows = pl.ds(i * size, size)
        product = dot3(inc_v[rows, :] * std_v[rows, :], vhi, vlo)
        for h in HALF:
            work[h, rows, :] = product[:, h * LANES:(h + 1) * LANES]

    pl.semaphore_wait(barrier, CHIPS + LATS - 1)
    send(segco.at[core], segco.at[core], 0, partner)

    def lon_sweeps(half, put):
        first = half * (ROWS // 2)
        rows = lambda i: pl.ds(first + i, 32, stride=NLON)
        for k in STATES:
            ys = [jnp.zeros((32, LANES), F32)] * 2
            for i in range(NLON) if k % 2 == 0 else reversed(range(NLON)):
                for h in HALF:
                    u = work[h, rows(i), :] if k == 0 else temp[h, i]
                    d = lon_row(i, h)
                    ys[h] = d * ys[h] + (1.0 - d) * u
                    if k < 3:
                        temp[h, i] = ys[h]
                    else:
                        work[h, rows(i), :] = ys[h]
            for h in HALF:
                put(h, k, ys[h])

    def put_out(h, k, y):
        pair_out[h, k] = y

    def put_own(h, k, y):
        seg[core, h, k] = y

    lon_sweeps(other, put_out)
    send(pair_out, seg.at[core], 1, partner)

    arrived(segco.at[other], 0)
    co = lambda s, h, r: segco[s, h, pl.ds(r, 1), :]
    for h in HALF:
        g_l, a21_l, a32_l, a31_l, a42_l, a41_l = (co(0, h, r) for r in range(6))
        g_r, a21_r, a32_r, a31_r, a42_r, a41_r = (co(1, h, r) for r in range(6))
        b1 = a21_r * g_l
        f2 = a32_l * b1 + a31_l
        b2 = a21_r * f2 + a41_r * g_l
        f2b = a32_l * g_r
        values = (
            g_l * g_r,
            g_l * b1 + a21_l,
            g_r * f2b + a32_r,
            g_r * f2 + a31_r * g_l,
            g_l * (a21_r * f2b + a42_r) + a42_l * g_r,
            g_l * b2 + a42_l * b1 + a41_l,
        )
        for r, value in enumerate(values):
            chipco[h, pl.ds(r, 1), :] = value
        chipco[h, pl.ds(6, 2), :] = jnp.zeros((2, LANES), F32)
    coin[0] = chipco[chip // 8]
    for k in range(1, CHIPS):
        send(chipco.at[chip_at(k) // 8], coin.at[CHIPS - k], 2, peer(k))

    lon_sweeps(core, put_own)

    arrived(seg.at[other], 1)
    for h in HALF:
        g_l, a21_l, a32_l, a31_l, a42_l, a41_l = (co(0, h, r) for r in range(6))
        g_r, a21_r, a32_r, a31_r, a42_r, a41_r = (co(1, h, r) for r in range(6))
        l1, l2, l3, l4 = (seg[0, h, k] for k in STATES)
        r1, r2, r3, r4 = (seg[1, h, k] for k in STATES)
        b1 = a21_r * l1 + r2
        f2 = a32_l * b1 + l3
        b2 = a21_r * f2 + a41_r * l1 + r4
        merged = (
            g_r * l1 + r1,
            g_l * b1 + l2,
            g_r * f2 + a31_r * l1 + r3,
            g_l * b2 + a42_l * b1 + l4,
        )
        for k in STATES:
            for j in range(8):
                s_out[8 * h + j, k] = merged[k][4 * j:4 * j + 4]
    for k in range(1, CHIPS):
        send(s_out.at[chip_at(k)], s_in.at[CHIPS - k], 3, peer(k))
    s_in[0] = s_out[chip]

    loads[2].wait()
    latu[...] = jnp.zeros_like(latu)

    def lat_sweep(lines, reverse, carry):
        def body(step, ys):
            ys = list(ys)
            first = pl.multiple_of((NLAT // 8 - 1 - step if reverse else step) * 8, 8)
            decays = [latd_v[pl.ds(first, 8), lanes(h)] for h in HALF]
            for j in reversed(range(8)) if reverse else range(8):
                i = first + j
                for n, (ref, h, height) in enumerate(lines):
                    d = decays[h][j:j + 1]
                    at = pl.ds(pl.multiple_of(i * height, height), height)
                    ys[n] = d * ys[n] + (1.0 - d) * ref[h, at, :]
                    ref[h, at, :] = ys[n]
            return tuple(ys)

        return lax.fori_loop(0, NLAT // 8, body, tuple(carry))

    lines = [(work, 0, 16), (work, 1, 16), (latu, 0, 8), (latu, 1, 8)]
    ends = []
    for k in STATES:
        start = [jnp.zeros((16, LANES), F32)] * 2 + [one_hot(k)] * 2
        ends.append(lat_sweep(lines, k % 2 == 1, start))
    for h in HALF:
        for k in STATES:
            latz[lat, h, pl.ds(16 * k, 16), :] = ends[k][h]
        store_coefs(latz, (lat, h), 64, [e[2 + h] for e in ends])
    for k in range(1, LATS):
        send(latz.at[lat], latz.at[lat], 4, lat_peer(k))

    arrived(coin.at[pl.ds(1, CHIPS - 1)], 2)
    cc = [[coin[j, pl.ds(r, 1), :] for r in range(6)] for j in range(CHIPS)]
    ahead, behind = [jnp.ones((1, LANES), F32)], [jnp.ones((1, LANES), F32)]
    for j in range(CHIPS):
        ahead.append(ahead[-1] * cc[j][0])
        behind.append(behind[-1] * cc[CHIPS - 1 - j][0])
    close = 1.0 / (1.0 - ahead[CHIPS])
    arrived(s_in.at[pl.ds(1, CHIPS - 1)], 3)

    def ring(terms, reverse):
        t = jnp.zeros((4, LANES), F32)
        before = [None] * CHIPS
        order = range(CHIPS - 1, -1, -1) if reverse else range(CHIPS)
        for j in order:
            before[j] = t
            t = cc[j][0] * t + terms[j]
        start = t * close
        growth = (lambda j: behind[CHIPS - 1 - j]) if reverse else (lambda j: ahead[j])
        return [before[j] + growth(j) * start for j in range(CHIPS)]

    seat = range(CHIPS)
    x1 = ring([s_in[j, 0] for j in seat], False)
    x2 = ring([s_in[j, 1] + cc[j][1] * x1[j] for j in seat], True)
    x3 = ring([s_in[j, 2] + cc[j][3] * x1[j] + cc[j][2] * x2[j] for j in seat], False)
    x4 = ring([s_in[j, 3] + cc[j][5] * x1[j] + cc[j][4] * x2[j] + cc[j][1] * x3[j] for j in seat], True)
    for j in seat:
        for k, x in enumerate((x1, x2, x3, x4)):
            x_out[j, k] = x[j]
    for k in range(1, CHIPS):
        send(x_out.at[k], x_in.at[chip], 5, peer(k))
    x_in[chip] = x_out[0]

    adj[...] = jnp.zeros_like(adj)

    def adjoint(reverse, carry):
        def body(step, cs):
            cs = list(cs)
            first = pl.multiple_of((NLAT // 8 - 1 - step if reverse else step) * 8, 8)
            decays = [latd_v[pl.ds(first, 8), lanes(h)] for h in HALF]
            for j in reversed(range(8)) if reverse else range(8):
                at = pl.ds(pl.multiple_of((first + j) * 8, 8), 8)
                for h in HALF:
                    d = decays[h][j:j + 1]
                    t = adj[h, at, :] + cs[h]
                    adj[h, at, :] = (1.0 - d) * t
                    cs[h] = d * t
            return tuple(cs)

        lax.fori_loop(0, NLAT // 8, body, tuple(carry))

    for k in (3, 2, 1, 0):
        adjoint(k % 2 == 0, [one_hot(k)] * 2)

    def lat_solve(state, coef, put, zero):
        x1, x2, x3, x4 = ([zero] * LATS for _ in STATES)
        for p in range(LATS - 1):
            x1[p + 1] = coef(p, 0) * x1[p] + state(p, 0)
        for p in range(LATS - 1, 0, -1):
            x2[p - 1] = coef(p, 0) * x2[p] + (coef(p, 1) * x1[p] + state(p, 1))
        for p in range(LATS - 1):
            x3[p + 1] = coef(p, 0) * x3[p] + (coef(p, 2) * x2[p] + coef(p, 3) * x1[p] + state(p, 2))
        for p in range(LATS - 1, 0, -1):
            x4[p - 1] = coef(p, 0) * x4[p] + (
                coef(p, 1) * x3[p] + coef(p, 4) * x2[p] + coef(p, 5) * x1[p] + state(p, 3)
            )
        for p in range(LATS):
            for k, x in enumerate((x1, x2, x3, x4)):
                put(p, k, x[p])

    arrived(latz.at[pl.ds(0, LATS - 1)], 4)
    for h in HALF:
        def put_z(p, k, x, h=h):
            latx[p, h, pl.ds(16 * k, 16), :] = x

        lat_solve(
            lambda p, k: latz[p, h, pl.ds(16 * k, 16), :],
            lambda p, r: latz[p, h, pl.ds(64 + r, 1), :],
            put_z, jnp.zeros((16, LANES), F32),
        )

    arrived(x_in.at[pl.ds(0, CHIPS - 1)], 5)
    for h in HALF:
        g_l, a21_l, a32_l, a31_l, a42_l, a41_l = (co(0, h, r) for r in range(6))
        g_r, a21_r, a32_r, a31_r, a42_r, a41_r = (co(1, h, r) for r in range(6))
        l1, l2, l3, l4 = (seg[0, h, k] for k in STATES)
        r1, r2, r3, r4 = (seg[1, h, k] for k in STATES)
        e1, e2, e3, e4 = (jnp.concatenate([x_in[8 * h + j, k] for j in range(8)], axis=0) for k in STATES)
        f1 = g_l * e1 + l1
        b1 = g_r * e2 + a21_r * f1 + r2
        f2 = g_l * e3 + a32_l * b1 + a31_l * e1 + l3
        b2 = g_r * e4 + a21_r * f2 + a42_r * e2 + a41_r * f1 + r4
        for k, (left, right) in enumerate(((e1, f1), (b1, e2), (e3, f2), (b2, e4))):
            unm[0, h, k] = left
            unm[1, h, k] = right
    send(unm.at[other], xlon.at[core], 6, partner)
    xlon[core] = unm[core]
    xcol[...] = jnp.zeros_like(xcol)
    arrived(xlon.at[other], 6)

    for h in HALF:
        for k in STATES:
            weights = adj[h, pl.ds(k, NLAT, stride=8), :]
            for c in STATES:
                total = weights[0:32] * xlon[0, h, c] + weights[32:64] * xlon[1, h, c]
                latc[lat, h, pl.ds(4 * k + c, 1), :] = jnp.sum(total, axis=0, keepdims=True)
    for k in range(1, LATS):
        send(latc.at[lat], latc.at[lat], 7, lat_peer(k))

    for h in HALF:
        for half in range(2):
            for c in STATES:
                xcol[h, pl.ds(256 * half + c, 32, stride=8), :] = xlon[half, h, c]
    lines = [(xcol, 0, 8), (xcol, 1, 8)]
    for k in STATES:
        lat_sweep(lines, k % 2 == 1, [jnp.zeros((8, LANES), F32)] * 2)
    lon_unit = [[lonu[h, pl.ds(c, NLON, stride=8), :] for c in STATES] for h in HALF]

    def add_lon(step, _):
        for j in range(4):
            i = step * 4 + j
            for h in HALF:
                at = pl.ds(pl.multiple_of(i * 16, 16), 16)
                y = work[h, at, :]
                column = xcol[h, pl.ds(pl.multiple_of(i * 8, 8), 8), :]
                for c in STATES:
                    y = y + column[c:c + 1] * lon_unit[h][c]
                work[h, at, :] = y
        return 0

    lax.fori_loop(0, NLAT // 4, add_lon, 0)

    arrived(latc.at[pl.ds(0, LATS - 1)], 7)
    enter = []
    for h in HALF:
        def put_c(p, k, x, h=h):
            latcx[p, h, pl.ds(4 * k, 4), :] = x

        lat_solve(
            lambda p, k: latc[p, h, pl.ds(4 * k, 4), :],
            lambda p, r: latz[p, h, pl.ds(64 + r, 1), :],
            put_c, jnp.zeros((4, LANES), F32),
        )
        for k in STATES:
            x = latx[lat, h, pl.ds(16 * k, 16), :]
            for c in STATES:
                x = x + lon_unit[h][c] * latcx[lat, h, pl.ds(4 * k + c, 1), :]
            enter.append(x)

    def finish(step, _):
        for h in HALF:
            for j in range(8):
                i = step * 8 + j
                at = pl.ds(pl.multiple_of(i * 16, 16), 16)
                y = work[h, at, :]
                unit = latu[h, pl.ds(pl.multiple_of(i * 8, 8), 8), :]
                for k in STATES:
                    y = y + unit[k:k + 1] * enter[4 * h + k]
                inc_v[at, lanes(h)] = y
        rows = pl.ds(pl.multiple_of(step * 128, 128), 128)
        out_v[rows, :] = std_v[rows, :] * dot3(inc_v[rows, :], thi, tlo)
        pltpu.make_async_copy(out_v.at[rows], out.at[rows], osem.at[0]).start()
        return 0

    lax.fori_loop(0, 8, finish, 0)
    pltpu.make_async_copy(out_v, out, osem.at[0]).wait()
    sent(segco.at[core], 0)
    sent(pair_out, 1)
    sent(coin.at[pl.ds(1, CHIPS - 1)], 2)
    sent(s_in.at[pl.ds(1, CHIPS - 1)], 3)
    sent(latz.at[pl.ds(0, LATS - 1)], 4)
    sent(x_in.at[pl.ds(0, CHIPS - 1)], 5)
    sent(unm.at[other], 6)
    sent(latc.at[pl.ds(0, LATS - 1)], 7)


def per_device(increment, error_std, vertical, lon_decay, lat_decay):
    vmem = lambda *shape: pltpu.VMEM(shape, F32)
    result = pl.pallas_call(
        kernel,
        out_shape=jax.ShapeDtypeStruct((ROWS, 256), F32),
        in_specs=[pl.BlockSpec(memory_space=pl.ANY)] * 5,
        out_specs=pl.BlockSpec(memory_space=pl.ANY),
        scratch_shapes=[
            vmem(ROWS, 256), vmem(ROWS, 256), vmem(4, 64, 64), vmem(NLON, 256), vmem(NLAT, 256), vmem(ROWS, 256),
            *[pltpu.VMEM((256, 256), BF16)] * 4,
            vmem(2, ROWS, LANES), vmem(2, NLON, 32, LANES), vmem(2, NLON * 8, LANES),
            *[vmem(2, NLAT * 8, LANES)] * 3,
            vmem(2, 4, 32, LANES), vmem(2, 2, 4, 32, LANES), vmem(2, 2, 8, LANES), vmem(2, 8, LANES), vmem(CHIPS, 8, LANES),
            *[vmem(CHIPS, 4, 4, LANES)] * 4,
            vmem(2, 2, 4, 32, LANES), vmem(2, 2, 4, 32, LANES),
            vmem(LATS, 2, 72, LANES), vmem(LATS, 2, 16, LANES), vmem(LATS, 2, 64, LANES), vmem(LATS, 2, 16, LANES),
            pltpu.SemaphoreType.DMA((11,)), pltpu.SemaphoreType.DMA((1,)),
            pltpu.SemaphoreType.DMA((8,)), pltpu.SemaphoreType.DMA((8,)),
        ],
        compiler_params=pltpu.CompilerParams(
            collective_id=0, has_side_effects=True, vmem_limit_bytes=24 * 1024 * 1024
        ),
    )(*[
        pltpu.with_memory_space_constraint(x, pltpu.HBM)
        for x in (increment.reshape(ROWS, 256), error_std.reshape(ROWS, 256), vertical, lon_decay, lat_decay)
    ])
    return result.reshape(NLAT, NLON, 256)


def solution(mesh):
    placed = (P("lat", "lon", None), P("lat", "lon", None), P(), P("lon", None), P("lat", None))
    return jax.shard_map(
        per_device, mesh=mesh, in_specs=placed, out_specs=P("lat", "lon", None), check_vma=False
    )
```

time: 1740 us -> 39.4 us (0.02)
  the two profiles are of different devices: /device:TPU:2 before, /device:TPU:1 now
where the time goes in v1:
time: 39.4 us; the launch traced here: 39.2 us
  Pallas kernels  38.2 us (97%)
  local copies, waits for them, and re-layouts  0.97 us (2%)
    pallas_call x1, Pallas kernels, per_device(): pl.pallas_call(kernel, out_shape=jax.ShapeDtypeStruct((ROWS, 256), F32),...  38.2 us
    unnamed x1, local copies, waits for them, and re-layouts  0.97 us

profile of v1, /device:TPU:1, one launch (start us, length us, event | category | flops | bytes accessed | tf_op | source)
XLA Modules:
  0.0 39.2 jit_solution(8514259209632534258)
XLA Ops:
  0.0 38.2 %shard_map.55 = f32[1024,256]{1,0:T(8,128)S(1)} custom-call(f32[1024,256]{1,0:T(8,128)} %bitcast.4, f32[1024,256]{1,0:T(8,128)} %bitcast.5, f32[4,64,64]{2,1,0:T(8,128)} %vert.1, f32[16,256]{1,0:T(8,128)} %lond.1, f32[64,256]{1,0:T(8,128)} %latd.1), custom_call_target="tpu_custom_call" | custom-call | tf_op jit(solution)/shard_map/pallas_call | solution.py:417
  38.2 1.0 %copy.7 = f32[64,16,256]{2,1,0:T(8,128)} copy(f32[64,16,256]{2,1,0:T(8,128)S(1)} %bitcast.3) | data formatting | bytes 2097152

commit v2 on v1

--- a/solution.py
+++ b/solution.py
@@ -11,6 +11,8 @@
 NLAT, NLON, LANES = 64, 16, 128
 ROWS = NLAT * NLON
 CHIPS, LATS = 16, 8
+FAR_CHIPS = sorted(range(1, CHIPS), key=lambda k: -min(k, CHIPS - k))
+FAR_LATS = sorted(range(1, LATS), key=lambda k: -min(k, LATS - k))
 HALF = range(2)
 STATES = range(4)
 
@@ -23,7 +25,9 @@
 def dot3(x, high_ref, low_ref):
     high, low = split(x)
     dot = lambda a, b: jnp.dot(a, b, preferred_element_type=F32)
-    return dot(high, high_ref[...]) + (dot(low, high_ref[...]) + dot(high, low_ref[...]))
+    rows = x.shape[0]
+    both = dot(jnp.concatenate([high, low], axis=0), high_ref[...])
+    return both[:rows] + (both[rows:] + dot(high, low_ref[...]))
 
 
 def one_hot(k):
@@ -38,13 +42,14 @@
 
 
 def kernel(
-    inc, std, vert, lond, latd, out,
-    inc_v, std_v, vert_v, lond_v, latd_v, out_v,
-    vhi, vlo, thi, tlo, work, temp, lonu, latu, adj, xcol,
+    inc, std, vert, lond, latd,
+    work, latu, enter, std_v, thi, tlo,
+    inc_v, vert_v, lond_v, latd_v,
+    vhi, vlo, temp, lonu, adj, xcol,
     pair_out, seg, segco, chipco, coin,
     s_out, s_in, x_out, x_in, unm, xlon,
-    latz, latc, latx, latcx,
-    lsem, osem, ssem, rsem,
+    latz, latc, lato, latx, latcx,
+    lsem, ssem, rsem,
 ):
     lon, lat = lax.axis_index("lon"), lax.axis_index("lat")
     core, chip = lax.rem(lon, 2), lon // 2
@@ -53,13 +58,12 @@
     chip_at = lambda k: lax.rem(chip + k, CHIPS)
     peer = lambda k: {"lon": 2 * chip_at(k) + core}
     lat_peer = lambda k: {"lat": lax.rem(lat + k, LATS)}
+    cross_peer = lambda k: {"lon": 2 * chip + other, "lat": lax.rem(lat + k, LATS)}
 
     barrier = pltpu.get_barrier_semaphore()
-    pl.semaphore_signal(barrier, inc=1, device_id=partner, device_id_type=MESH)
-    for k in range(1, CHIPS):
-        pl.semaphore_signal(barrier, inc=1, device_id=peer(k), device_id_type=MESH)
-    for k in range(1, LATS):
-        pl.semaphore_signal(barrier, inc=1, device_id=lat_peer(k), device_id_type=MESH)
+    greeted = [peer(k) for k in FAR_CHIPS] + [p(k) for k in FAR_LATS for p in (lat_peer, cross_peer)] + [partner]
+    for device in greeted:
+        pl.semaphore_signal(barrier, inc=1, device_id=device, device_id_type=MESH)
 
     loads = [pltpu.make_async_copy(a, b, lsem.at[i]) for i, (a, b) in enumerate(((lond, lond_v), (vert, vert_v), (latd, latd_v)))]
     for copy in loads:
@@ -128,9 +132,6 @@
         product = dot3(inc_v[rows, :] * std_v[rows, :], vhi, vlo)
         for h in HALF:
             work[h, rows, :] = product[:, h * LANES:(h + 1) * LANES]
-
-    pl.semaphore_wait(barrier, CHIPS + LATS - 1)
-    send(segco.at[core], segco.at[core], 0, partner)
 
     def lon_sweeps(half, put):
         first = half * (ROWS // 2)
@@ -156,6 +157,8 @@
         seg[core, h, k] = y
 
     lon_sweeps(other, put_out)
+    pl.semaphore_wait(barrier, len(greeted))
+    send(segco.at[core], segco.at[core], 0, partner)
     send(pair_out, seg.at[core], 1, partner)
 
     arrived(segco.at[other], 0)
@@ -179,7 +182,7 @@
             chipco[h, pl.ds(r, 1), :] = value
         chipco[h, pl.ds(6, 2), :] = jnp.zeros((2, LANES), F32)
     coin[0] = chipco[chip // 8]
-    for k in range(1, CHIPS):
+    for k in FAR_CHIPS:
         send(chipco.at[chip_at(k) // 8], coin.at[CHIPS - k], 2, peer(k))
 
     lon_sweeps(core, put_own)
@@ -202,7 +205,7 @@
         for k in STATES:
             for j in range(8):
                 s_out[8 * h + j, k] = merged[k][4 * j:4 * j + 4]
-    for k in range(1, CHIPS):
+    for k in FAR_CHIPS:
         send(s_out.at[chip_at(k)], s_in.at[CHIPS - k], 3, peer(k))
     s_in[0] = s_out[chip]
 
@@ -234,7 +237,7 @@
         for k in STATES:
             latz[lat, h, pl.ds(16 * k, 16), :] = ends[k][h]
         store_coefs(latz, (lat, h), 64, [e[2 + h] for e in ends])
-    for k in range(1, LATS):
+    for k in FAR_LATS:
         send(latz.at[lat], latz.at[lat], 4, lat_peer(k))
 
     arrived(coin.at[pl.ds(1, CHIPS - 1)], 2)
@@ -265,7 +268,7 @@
     for j in seat:
         for k, x in enumerate((x1, x2, x3, x4)):
             x_out[j, k] = x[j]
-    for k in range(1, CHIPS):
+    for k in FAR_CHIPS:
         send(x_out.at[k], x_in.at[chip], 5, peer(k))
     x_in[chip] = x_out[0]
 
@@ -332,19 +335,24 @@
             unm[0, h, k] = left
             unm[1, h, k] = right
     send(unm.at[other], xlon.at[core], 6, partner)
+
+    weights = [[adj[h, pl.ds(256 * core + k, 32, stride=8), :] for k in STATES] for h in HALF]
+    for whose, put in ((other, lambda h, r: lato.at[h, pl.ds(r, 1)]), (core, lambda h, r: latc.at[2 * lat + core, h, pl.ds(r, 1)])):
+        for h in HALF:
+            for c in STATES:
+                x = unm[whose, h, c]
+                for k in STATES:
+                    put(h, 4 * k + c)[...] = jnp.sum(weights[h][k] * x, axis=0, keepdims=True)
+        for k in FAR_LATS:
+            if whose is other:
+                send(lato, latc.at[2 * lat + core], 7, cross_peer(k))
+            else:
+                send(latc.at[2 * lat + core], latc.at[2 * lat + core], 7, lat_peer(k))
+    send(lato, latc.at[2 * lat + core], 7, partner)
+
     xlon[core] = unm[core]
     xcol[...] = jnp.zeros_like(xcol)
     arrived(xlon.at[other], 6)
-
-    for h in HALF:
-        for k in STATES:
-            weights = adj[h, pl.ds(k, NLAT, stride=8), :]
-            for c in STATES:
-                total = weights[0:32] * xlon[0, h, c] + weights[32:64] * xlon[1, h, c]
-                latc[lat, h, pl.ds(4 * k + c, 1), :] = jnp.sum(total, axis=0, keepdims=True)
-    for k in range(1, LATS):
-        send(latc.at[lat], latc.at[lat], 7, lat_peer(k))
-
     for h in HALF:
         for half in range(2):
             for c in STATES:
@@ -368,14 +376,13 @@
 
     lax.fori_loop(0, NLAT // 4, add_lon, 0)
 
-    arrived(latc.at[pl.ds(0, LATS - 1)], 7)
-    enter = []
+    arrived(latc.at[pl.ds(0, 2 * LATS - 1)], 7)
     for h in HALF:
         def put_c(p, k, x, h=h):
             latcx[p, h, pl.ds(4 * k, 4), :] = x
 
         lat_solve(
-            lambda p, k: latc[p, h, pl.ds(4 * k, 4), :],
+            lambda p, k: latc[2 * p, h, pl.ds(4 * k, 4), :] + latc[2 * p + 1, h, pl.ds(4 * k, 4), :],
             lambda p, r: latz[p, h, pl.ds(64 + r, 1), :],
             put_c, jnp.zeros((4, LANES), F32),
         )
@@ -383,25 +390,8 @@
             x = latx[lat, h, pl.ds(16 * k, 16), :]
             for c in STATES:
                 x = x + lon_unit[h][c] * latcx[lat, h, pl.ds(4 * k + c, 1), :]
-            enter.append(x)
-
-    def finish(step, _):
-        for h in HALF:
-            for j in range(8):
-                i = step * 8 + j
-                at = pl.ds(pl.multiple_of(i * 16, 16), 16)
-                y = work[h, at, :]
-                unit = latu[h, pl.ds(pl.multiple_of(i * 8, 8), 8), :]
-                for k in STATES:
-                    y = y + unit[k:k + 1] * enter[4 * h + k]
-                inc_v[at, lanes(h)] = y
-        rows = pl.ds(pl.multiple_of(step * 128, 128), 128)
-        out_v[rows, :] = std_v[rows, :] * dot3(inc_v[rows, :], thi, tlo)
-        pltpu.make_async_copy(out_v.at[rows], out.at[rows], osem.at[0]).start()
-        return 0
-
-    lax.fori_loop(0, 8, finish, 0)
-    pltpu.make_async_copy(out_v, out, osem.at[0]).wait()
+            enter[h, k] = x
+
     sent(segco.at[core], 0)
     sent(pair_out, 1)
     sent(coin.at[pl.ds(1, CHIPS - 1)], 2)
@@ -409,27 +399,52 @@
     sent(latz.at[pl.ds(0, LATS - 1)], 4)
     sent(x_in.at[pl.ds(0, CHIPS - 1)], 5)
     sent(unm.at[other], 6)
-    sent(latc.at[pl.ds(0, LATS - 1)], 7)
+    sent(latc.at[pl.ds(0, 2 * LATS - 1)], 7)
+
+
+def finish(work, latu, enter, std, thi, tlo, out, line, out_v, sem):
+    parts = 4
+    size = ROWS // parts
+
+    def part(step, _):
+        for h in HALF:
+            for j in range(size // 16):
+                i = step * (size // 16) + j
+                y = work[h, pl.ds(pl.multiple_of(i * 16, 16), 16), :]
+                unit = latu[h, pl.ds(pl.multiple_of(i * 8, 8), 8), :]
+                for k in STATES:
+                    y = y + unit[k:k + 1] * enter[h, k]
+                line[pl.ds(16 * j, 16), pl.ds(h * LANES, LANES)] = y
+        rows = pl.ds(pl.multiple_of(step * size, size), size)
+        out_v[rows, :] = std[rows, :] * dot3(line[...], thi, tlo)
+        pltpu.make_async_copy(out_v.at[rows], out.at[rows], sem.at[0]).start()
+        return 0
+
+    lax.fori_loop(0, parts, part, 0)
+    pltpu.make_async_copy(out_v, out, sem.at[0]).wait()
 
 
 def per_device(increment, error_std, vertical, lon_decay, lat_decay):
     vmem = lambda *shape: pltpu.VMEM(shape, F32)
-    result = pl.pallas_call(
+    whole = pl.BlockSpec(memory_space=pltpu.VMEM)
+    square = pltpu.VMEM((256, 256), BF16)
+    held = pl.pallas_call(
         kernel,
-        out_shape=jax.ShapeDtypeStruct((ROWS, 256), F32),
+        out_shape=[
+            vmem(2, ROWS, LANES), vmem(2, NLAT * 8, LANES), vmem(2, 4, NLON, LANES), vmem(ROWS, 256), square, square,
+        ],
         in_specs=[pl.BlockSpec(memory_space=pl.ANY)] * 5,
-        out_specs=pl.BlockSpec(memory_space=pl.ANY),
+        out_specs=[whole] * 6,
         scratch_shapes=[
-            vmem(ROWS, 256), vmem(ROWS, 256), vmem(4, 64, 64), vmem(NLON, 256), vmem(NLAT, 256), vmem(ROWS, 256),
-            *[pltpu.VMEM((256, 256), BF16)] * 4,
-            vmem(2, ROWS, LANES), vmem(2, NLON, 32, LANES), vmem(2, NLON * 8, LANES),
-            *[vmem(2, NLAT * 8, LANES)] * 3,
+            vmem(ROWS, 256), vmem(4, 64, 64), vmem(NLON, 256), vmem(NLAT, 256),
+            square, square, vmem(2, NLON, 32, LANES), vmem(2, NLON * 8, LANES),
+            *[vmem(2, NLAT * 8, LANES)] * 2,
             vmem(2, 4, 32, LANES), vmem(2, 2, 4, 32, LANES), vmem(2, 2, 8, LANES), vmem(2, 8, LANES), vmem(CHIPS, 8, LANES),
             *[vmem(CHIPS, 4, 4, LANES)] * 4,
             vmem(2, 2, 4, 32, LANES), vmem(2, 2, 4, 32, LANES),
-            vmem(LATS, 2, 72, LANES), vmem(LATS, 2, 16, LANES), vmem(LATS, 2, 64, LANES), vmem(LATS, 2, 16, LANES),
-            pltpu.SemaphoreType.DMA((11,)), pltpu.SemaphoreType.DMA((1,)),
-            pltpu.SemaphoreType.DMA((8,)), pltpu.SemaphoreType.DMA((8,)),
+            vmem(LATS, 2, 72, LANES), vmem(2 * LATS, 2, 16, LANES), vmem(2, 16, LANES),
+            vmem(LATS, 2, 64, LANES), vmem(LATS, 2, 16, LANES),
+            pltpu.SemaphoreType.DMA((11,)), pltpu.SemaphoreType.DMA((8,)), pltpu.SemaphoreType.DMA((8,)),
         ],
         compiler_params=pltpu.CompilerParams(
             collective_id=0, has_side_effects=True, vmem_limit_bytes=24 * 1024 * 1024
@@ -438,6 +453,14 @@
         pltpu.with_memory_space_constraint(x, pltpu.HBM)
         for x in (increment.reshape(ROWS, 256), error_std.reshape(ROWS, 256), vertical, lon_decay, lat_decay)
     ])
+    result = pl.pallas_call(
+        finish,
+        out_shape=jax.ShapeDtypeStruct((ROWS, 256), F32),
+        in_specs=[whole] * 6,
+        out_specs=pl.BlockSpec(memory_space=pl.ANY),
+        scratch_shapes=[vmem(256, 256), vmem(ROWS, 256), pltpu.SemaphoreType.DMA((1,))],
+        compiler_params=pltpu.CompilerParams(vmem_limit_bytes=24 * 1024 * 1024),
+    )(*held)
     return result.reshape(NLAT, NLON, 256)
 
 

time: 39.4 us -> 34.5 us (0.88)
  Pallas kernels: 38.2 us -> 34.4 us
  local copies, waits for them, and re-layouts: 0.97 us -> 0 us
    pallas_call x1 -> x2, Pallas kernels: 38.2 us -> 34.4 us  [the longest x1 32.5 us: per_device(): pl.pallas_call(kernel, out_shape=[vmem(2, ROWS, LANES), vmem(2, NLAT * 8,...]
    unnamed x1 -> x0, local copies, waits for them, and re-layouts: 0.97 us -> none
where the time goes in v2:
time: 34.5 us; the launch traced here: 34.4 us
  Pallas kernels  34.4 us (100%)
    pallas_call x1, Pallas kernels, per_device(): pl.pallas_call(kernel, out_shape=[vmem(2, ROWS, LANES), vmem(2, NLAT * 8,...  32.5 us
    pallas_call x1, Pallas kernels, per_device(): pl.pallas_call(finish, out_shape=jax.ShapeDtypeStruct((ROWS, 256), F32),...  1.9 us

profile of v2, /device:TPU:1, one launch (start us, length us, event | category | flops | bytes accessed | tf_op | source)
XLA Modules:
  0.0 34.4 jit_solution(4857607191621449469)
XLA Ops:
  0.0 32.5 %shard_map.55 = (f32[2,1024,128]{2,1,0:T(8,128)S(1)}, f32[2,512,128]{2,1,0:T(8,128)S(1)}, f32[2,4,16,128]{3,2,1,0:T(8,128)S(1)}, f32[1024,256]{1,0:T(8,128)S(1)}...) custom-call(f32[1024,256]{1,0:T(8,128)} %bitcast.3, f32[1024,256]{1,0:T(8,128)} %bitcast.4, ...), custom_call_target="tpu_custom_call" | custom-call | tf_op jit(solution)/shard_map/pallas_call | solution.py:431
  32.5 1.9 %shard_map.56 = f32[1024,256]{1,0:T(8,128)} custom-call(f32[2,1024,128]{2,1,0:T(8,128)S(1)} %get-tuple-element.11.work, f32[2,512,128]{2,1,0:T(8,128)S(1)} %get-tuple-element.12.latu, f32[2,4,16,128]{3,2,1,0:T(8,128)S(1)} %get-tuple-element.13.enter, f32[1024,256]{1,0:T(8,128)S(1)} %get-tuple-element.14.std, bf16[256,256]{1,0:T(8,128)(2,1)S(1)} %get-tuple-element.15.thi, ...), custom_call_target="tpu_custom_call" | custom-call | tf_op jit(solution)/shard_map/pallas_call | solution.py:456

commit v3 on v2

v3 whole, which is shorter than its diff:
```python
import jax
import jax.numpy as jnp
from jax import lax
from jax.experimental import pallas as pl
from jax.experimental.pallas import tpu as pltpu
from jax.sharding import PartitionSpec as P

MESH = pl.DeviceIdType.MESH
F32 = jnp.float32
BF16 = jnp.bfloat16
NLAT, NLON, LANES = 64, 16, 128
ROWS = NLAT * NLON
LONS, CHIPS, LATS = 32, 16, 8
FAR_CHIPS = sorted(range(1, CHIPS), key=lambda k: -min(k, CHIPS - k))
FAR_LONS = sorted(range(1, LONS), key=lambda k: -min(k, LONS - k))
FAR_LATS = sorted(range(1, LATS), key=lambda k: -min(k, LATS - k))
HALF = range(2)
STATES = range(4)


def split(x):
    high = x.astype(BF16)
    return high, (x - high.astype(F32)).astype(BF16)


def dot3(x, weight):
    both = jnp.dot(jnp.concatenate(split(x), axis=1), weight, preferred_element_type=F32)
    return both[:, :LANES] + both[:, LANES:]


def one_hot(k):
    return jnp.where(lax.broadcasted_iota(jnp.int32, (8, LANES), 0) == k, 1.0, 0.0).astype(F32)


def store_coefs(ref, at, base, rows):
    for row, part in enumerate(rows):
        ref[(*at, pl.ds(base + row, 1), slice(None))] = part
    ref[(*at, pl.ds(base + 6, 2), slice(None))] = jnp.zeros((2, LANES), F32)


def kernel(
    inc, std, vert, lond, latd,
    work, latu, enter, std_v, tw,
    inc_v, vert_v, lond_v, latd_v,
    vw, temp, lonu, adj, xcol,
    pair_out, seg, segco, chipco, coin,
    s_out, s_in, x_out, x_in, unm, xlon,
    latc, latcx, lz_out, lz_in, lzx_out, lzx_in, sc_in, t_out, t_in, tx_out, tx_in,
    lsem, ssem, rsem,
):
    lon, lat = lax.axis_index("lon"), lax.axis_index("lat")
    core, chip = lax.rem(lon, 2), lon // 2
    other = 1 - core
    partner = {"lon": 2 * chip + other}
    chip_at = lambda k: lax.rem(chip + k, CHIPS)
    peer = lambda k: {"lon": 2 * chip_at(k) + core}
    lon_peer = lambda k: {"lon": lax.rem(lon + k, LONS)}
    lat_peer = lambda k: {"lat": lax.rem(lat + k, LATS)}

    barrier = pltpu.get_barrier_semaphore()
    greeted = [lon_peer(k) for k in FAR_LONS] + [lat_peer(k) for k in FAR_LATS]
    for device in greeted:
        pl.semaphore_signal(barrier, inc=1, device_id=device, device_id_type=MESH)

    loads = [pltpu.make_async_copy(a, b, lsem.at[i]) for i, (a, b) in enumerate(((lond, lond_v), (vert, vert_v), (latd, latd_v)))]
    for copy in loads:
        copy.start()
    parts = 4
    size = ROWS // parts
    big = []
    for i in range(parts):
        rows = pl.ds(i * size, size)
        big.append((
            pltpu.make_async_copy(inc.at[rows], inc_v.at[rows], lsem.at[3 + 2 * i]),
            pltpu.make_async_copy(std.at[rows], std_v.at[rows], lsem.at[4 + 2 * i]),
        ))
        for copy in big[-1]:
            copy.start()

    def send(src, dst, which, device):
        copy = pltpu.make_async_remote_copy(
            src_ref=src, dst_ref=dst, send_sem=ssem.at[which], recv_sem=rsem.at[which],
            device_id=device, device_id_type=MESH,
        )
        copy.start()

    def arrived(ref, which):
        pltpu.make_async_copy(ref, ref, rsem.at[which]).wait()

    def sent(ref, which):
        pltpu.make_async_copy(ref, ref, ssem.at[which]).wait()

    loads[0].wait()
    lanes = lambda h: pl.ds(h * LANES, LANES)
    lon_row = lambda i, h: lond_v[pl.ds(i, 1), lanes(h)]
    for h in HALF:
        ends = []
        line = [None] * NLON
        for k in STATES:
            y = one_hot(k)
            for i in range(NLON) if k % 2 == 0 else reversed(range(NLON)):
                d = lon_row(i, h)
                y = d * y if line[i] is None else d * y + (1.0 - d) * line[i]
                line[i] = y
            ends.append(y)
        for i in range(NLON):
            lonu[h, pl.ds(8 * i, 8), :] = line[i]
        e1, e2, e3, e4 = ends
        store_coefs(segco, (core, h), 0, (e1[0:1], e2[0:1], e3[1:2], e3[0:1], e4[1:2], e4[0:1]))

    loads[1].wait()
    zero64 = jnp.zeros((64, 64), F32)
    for p in range(2):
        a, b = vert_v[2 * p], vert_v[2 * p + 1]
        block = jnp.concatenate(
            [jnp.concatenate([a, zero64], axis=1), jnp.concatenate([zero64, b], axis=1)], axis=0
        )
        for factor, weight in ((block, vw), (block.T, tw)):
            high, low = split(factor)
            top = jnp.concatenate([high, low], axis=1)
            weight[p] = jnp.concatenate([top, jnp.concatenate([high, jnp.zeros_like(high)], axis=1)], axis=0)

    for i in range(parts):
        for copy in big[i]:
            copy.wait()
        rows = pl.ds(i * size, size)
        for h in HALF:
            work[h, rows, :] = dot3(inc_v[rows, lanes(h)] * std_v[rows, lanes(h)], vw[h])

    def lon_sweeps(half, put):
        first = half * (ROWS // 2)
        rows = lambda i: pl.ds(first + i, 32, stride=NLON)
        for k in STATES:
            ys = [jnp.zeros((32, LANES), F32)] * 2
            for i in range(NLON) if k % 2 == 0 else reversed(range(NLON)):
                for h in HALF:
                    u = work[h, rows(i), :] if k == 0 else temp[h, i]
                    d = lon_row(i, h)
                    ys[h] = d * ys[h] + (1.0 - d) * u
                    if k < 3:
                        temp[h, i] = ys[h]
                    else:
                        work[h, rows(i), :] = ys[h]
            for h in HALF:
                put(h, k, ys[h])

    def put_out(h, k, y):
        pair_out[h, k] = y

    def put_own(h, k, y):
        seg[core, h, k] = y

    lon_sweeps(other, put_out)
    pl.semaphore_wait(barrier, len(greeted))
    send(segco.at[core], segco.at[core], 0, partner)

    solves = lax.rem(lon, 8) // 2 == 1
    solvers = [(2 * k + h, h, 8 * k + 2 + h) for k in STATES for h in HALF]

    def to_solvers(out, into, which):
        for n, h, solver in solvers:
            place = lax.rem(lon - solver + LONS, LONS)

            @pl.when(place != 0)
            def _():
                send(out(n, h), into.at[place], which, {"lon": solver})

            @pl.when(place == 0)
            def _():
                into[0] = out(n, h)[...]

    to_solvers(lambda n, h: segco.at[core, h], sc_in, 8)
    send(pair_out, seg.at[core], 1, partner)

    loads[2].wait()
    adj[...] = jnp.zeros_like(adj)

    def adjoint(reverse, carry):
        def body(step, cs):
            cs = list(cs)
            first = pl.multiple_of((NLAT // 8 - 1 - step if reverse else step) * 8, 8)
            decays = [latd_v[pl.ds(first, 8), lanes(h)] for h in HALF]
            for j in reversed(range(8)) if reverse else range(8):
                at = pl.ds(pl.multiple_of((first + j) * 8, 8), 8)
                for h in HALF:
                    d = decays[h][j:j + 1]
                    t = adj[h, at, :] + cs[h]
                    adj[h, at, :] = (1.0 - d) * t
                    cs[h] = d * t
            return tuple(cs)

        return lax.fori_loop(0, NLAT // 8, body, tuple(carry))

    carried = [adjoint(k % 2 == 0, [one_hot(k)] * 2) for k in (3, 2, 1, 0)]
    for h in HALF:
        e1, e2 = carried[3][h], carried[2][h]
        store_coefs(latc, (lat, h), 16, (e1[0:1], e1[1:2], e2[2:3], e1[2:3], e2[3:4], e1[3:4]))

    arrived(segco.at[other], 0)
    co = lambda s, h, r: segco[s, h, pl.ds(r, 1), :]
    for h in HALF:
        g_l, a21_l, a32_l, a31_l, a42_l, a41_l = (co(0, h, r) for r in range(6))
        g_r, a21_r, a32_r, a31_r, a42_r, a41_r = (co(1, h, r) for r in range(6))
        b1 = a21_r * g_l
        f2 = a32_l * b1 + a31_l
        b2 = a21_r * f2 + a41_r * g_l
        f2b = a32_l * g_r
        values = (
            g_l * g_r,
            g_l * b1 + a21_l,
            g_r * f2b + a32_r,
            g_r * f2 + a31_r * g_l,
            g_l * (a21_r * f2b + a42_r) + a42_l * g_r,
            g_l * b2 + a42_l * b1 + a41_l,
        )
        for r, value in enumerate(values):
            chipco[h, pl.ds(r, 1), :] = value
        chipco[h, pl.ds(6, 2), :] = jnp.zeros((2, LANES), F32)
    coin[0] = chipco[chip // 8]
    for k in FAR_CHIPS:
        send(chipco.at[chip_at(k) // 8], coin.at[CHIPS - k], 2, peer(k))

    lon_sweeps(core, put_own)

    weights = [[[adj[h, pl.ds(256 * half + k, 32, stride=8), :] for k in STATES] for half in (core, other)] for h in HALF]
    for h in HALF:
        for c in STATES:
            own, rest = seg[core, h, c], pair_out[h, c]
            for k in STATES:
                total = weights[h][0][k] * own + weights[h][1][k] * rest
                latc[lat, h, pl.ds(4 * k + c, 1), :] = jnp.sum(total, axis=0, keepdims=True)
    for k in FAR_LATS:
        send(latc.at[lat], latc.at[lat], 7, lat_peer(k))

    arrived(seg.at[other], 1)
    def merge(h, left, right):
        g_l, a21_l, a32_l, a31_l, a42_l, a41_l = (co(0, h, r) for r in range(6))
        g_r, a21_r, a32_r, a31_r, a42_r, a41_r = (co(1, h, r) for r in range(6))
        (l1, l2, l3, l4), (r1, r2, r3, r4) = left, right
        b1 = a21_r * l1 + r2
        f2 = a32_l * b1 + l3
        b2 = a21_r * f2 + a41_r * l1 + r4
        return (
            g_r * l1 + r1,
            g_l * b1 + l2,
            g_r * f2 + a31_r * l1 + r3,
            g_l * b2 + a42_l * b1 + l4,
        )

    def unmerge(h, left, right, entering):
        g_l, a21_l, a32_l, a31_l, a42_l, a41_l = (co(0, h, r) for r in range(6))
        g_r, a21_r, a32_r, a31_r, a42_r, a41_r = (co(1, h, r) for r in range(6))
        (l1, l2, l3, l4), (r1, r2, r3, r4) = left, right
        e1, e2, e3, e4 = entering
        f1 = g_l * e1 + l1
        b1 = g_r * e2 + a21_r * f1 + r2
        f2 = g_l * e3 + a32_l * b1 + a31_l * e1 + l3
        b2 = g_r * e4 + a21_r * f2 + a42_r * e2 + a41_r * f1 + r4
        return (e1, b1, e3, b2), (f1, e2, f2, e4)

    states = lambda s, h: [seg[s, h, k] for k in STATES]
    for h in HALF:
        merged = merge(h, states(0, h), states(1, h))
        for k in STATES:
            for j in range(8):
                s_out[8 * h + j, k] = merged[k][4 * j:4 * j + 4]
    for k in FAR_CHIPS:
        send(s_out.at[chip_at(k)], s_in.at[CHIPS - k], 3, peer(k))
    s_in[0] = s_out[chip]

    latu[...] = jnp.zeros_like(latu)

    def lat_sweep(lines, reverse, carry):
        def body(step, ys):
            ys = list(ys)
            first = pl.multiple_of((NLAT // 8 - 1 - step if reverse else step) * 8, 8)
            decays = [latd_v[pl.ds(first, 8), lanes(h)] for h in HALF]
            for j in reversed(range(8)) if reverse else range(8):
                i = first + j
                for n, (ref, h, height) in enumerate(lines):
                    d = decays[h][j:j + 1]
                    at = pl.ds(pl.multiple_of(i * height, height), height)
                    ys[n] = d * ys[n] + (1.0 - d) * ref[h, at, :]
                    ref[h, at, :] = ys[n]
            return tuple(ys)

        return lax.fori_loop(0, NLAT // 8, body, tuple(carry))

    lines = [(work, 0, 16), (work, 1, 16), (latu, 0, 8), (latu, 1, 8)]
    ends = []
    for k in STATES:
        start = [jnp.zeros((16, LANES), F32)] * 2 + [one_hot(k)] * 2
        ends.append(lat_sweep(lines, k % 2 == 1, start))
    for n in range(LATS):
        for k in STATES:
            lz_out[n, k] = ends[k][n // 4][4 * (n % 4):4 * (n % 4) + 4]
    for k in FAR_LATS:
        send(lz_out.at[lax.rem(lat + k, LATS)], lz_in.at[lat], 4, lat_peer(k))
    lz_in[lat] = lz_out[lat]

    def lat_solve(state, coef, put, zero):
        x1, x2, x3, x4 = ([zero] * LATS for _ in STATES)
        for p in range(LATS - 1):
            x1[p + 1] = coef(p, 0) * x1[p] + state(p, 0)
        for p in range(LATS - 1, 0, -1):
            x2[p - 1] = coef(p, 0) * x2[p] + (coef(p, 1) * x1[p] + state(p, 1))
        for p in range(LATS - 1):
            x3[p + 1] = coef(p, 0) * x3[p] + (coef(p, 2) * x2[p] + coef(p, 3) * x1[p] + state(p, 2))
        for p in range(LATS - 1, 0, -1):
            x4[p - 1] = coef(p, 0) * x4[p] + (
                coef(p, 1) * x3[p] + coef(p, 4) * x2[p] + coef(p, 5) * x1[p] + state(p, 3)
            )
        for p in range(LATS):
            for k, x in enumerate((x1, x2, x3, x4)):
                put(p, k, x[p])

    arrived(latc.at[pl.ds(0, LATS - 1)], 7)
    for h in HALF:
        def put_c(p, k, x, h=h):
            latcx[p, h, pl.ds(4 * k, 4), :] = x

        lat_solve(
            lambda p, k: latc[p, h, pl.ds(4 * k, 4), :],
            lambda p, r: latc[p, h, pl.ds(16 + r, 1), :],
            put_c, jnp.zeros((4, LANES), F32),
        )
    for n, h, _ in solvers:
        t_out[n] = latcx[lat, h, pl.ds(4 * (n // 2), 4), :]
    to_solvers(lambda n, h: t_out.at[n], t_in, 9)

    seat = range(CHIPS)

    def ring_maps(seat, row):
        cc = [[row(j, r) for r in range(6)] for j in seat]
        ahead, behind = [jnp.ones((1, LANES), F32)], [jnp.ones((1, LANES), F32)]
        for j in seat:
            ahead.append(ahead[-1] * cc[j][0])
            behind.append(behind[-1] * cc[-1 - j][0])
        return cc, ahead, behind, 1.0 / (1.0 - ahead[-1])

    def ring_solve(seat, maps, state, zero):
        cc, ahead, behind, close = maps

        def ring(terms, reverse):
            t = zero
            before = [None] * len(seat)
            for j in reversed(seat) if reverse else seat:
                before[j] = t
                t = cc[j][0] * t + terms[j]
            start = t * close
            growth = (lambda j: behind[len(seat) - 1 - j]) if reverse else (lambda j: ahead[j])
            return [before[j] + growth(j) * start for j in seat]

        x1 = ring([state(j, 0) for j in seat], False)
        x2 = ring([state(j, 1) + cc[j][1] * x1[j] for j in seat], True)
        x3 = ring([state(j, 2) + cc[j][3] * x1[j] + cc[j][2] * x2[j] for j in seat], False)
        x4 = ring([state(j, 3) + cc[j][5] * x1[j] + cc[j][4] * x2[j] + cc[j][1] * x3[j] for j in seat], True)
        return x1, x2, x3, x4

    arrived(coin.at[pl.ds(1, CHIPS - 1)], 2)
    maps = ring_maps(seat, lambda j, r: coin[j, pl.ds(r, 1), :])
    arrived(s_in.at[pl.ds(1, CHIPS - 1)], 3)
    x1, x2, x3, x4 = ring_solve(seat, maps, lambda j, k: s_in[j, k], jnp.zeros((4, LANES), F32))
    for j in seat:
        for k, x in enumerate((x1, x2, x3, x4)):
            x_out[j, k] = x[j]
    for k in FAR_CHIPS:
        send(x_out.at[k], x_in.at[chip], 5, peer(k))
    x_in[chip] = x_out[0]

    @pl.when(solves)
    def _():
        devices = range(LONS)
        arrived(sc_in.at[pl.ds(1, LONS - 1)], 8)
        maps = ring_maps(devices, lambda j, r: sc_in[j, pl.ds(r, 1), :])
        arrived(t_in.at[pl.ds(1, LONS - 1)], 9)
        found = ring_solve(devices, maps, lambda j, c: t_in[j, pl.ds(c, 1), :], jnp.zeros((1, LANES), F32))
        for j in devices:
            for c in STATES:
                tx_out[j, pl.ds(c, 1), :] = found[c][j]
        for k in FAR_LONS:
            send(tx_out.at[k], tx_in.at[2 * (lon // 8) + core], 10, lon_peer(k))
        tx_in[2 * (lon // 8) + core] = tx_out[0]

    arrived(lz_in.at[pl.ds(0, LATS - 1)], 4)

    def put_z(p, k, x):
        lzx_out[p, k] = x

    lat_solve(
        lambda p, k: lz_in[p, k],
        lambda p, r: latc[p, lat // 4, pl.ds(16 + r, 1), :],
        put_z, jnp.zeros((4, LANES), F32),
    )
    for k in FAR_LATS:
        send(lzx_out.at[lax.rem(lat + k, LATS)], lzx_in.at[lat], 11, lat_peer(k))
    lzx_in[lat] = lzx_out[lat]

    arrived(x_in.at[pl.ds(0, CHIPS - 1)], 5)
    for h in HALF:
        entering = [jnp.concatenate([x_in[8 * h + j, k] for j in range(8)], axis=0) for k in STATES]
        for whose, parts_in in enumerate(unmerge(h, states(0, h), states(1, h), entering)):
            for k in STATES:
                unm[whose, h, k] = parts_in[k]
    send(unm.at[other], xlon.at[core], 6, partner)

    xlon[core] = unm[core]
    xcol[...] = jnp.zeros_like(xcol)
    arrived(xlon.at[other], 6)
    for h in HALF:
        for half in range(2):
            for c in STATES:
                xcol[h, pl.ds(256 * half + c, 32, stride=8), :] = xlon[half, h, c]
    lines = [(xcol, 0, 8), (xcol, 1, 8)]
    for k in STATES:
        lat_sweep(lines, k % 2 == 1, [jnp.zeros((8, LANES), F32)] * 2)
    lon_unit = [[lonu[h, pl.ds(c, NLON, stride=8), :] for c in STATES] for h in HALF]

    def add_lon(step, _):
        for j in range(4):
            i = step * 4 + j
            for h in HALF:
                at = pl.ds(pl.multiple_of(i * 16, 16), 16)
                y = work[h, at, :]
                column = xcol[h, pl.ds(pl.multiple_of(i * 8, 8), 8), :]
                for c in STATES:
                    y = y + column[c:c + 1] * lon_unit[h][c]
                work[h, at, :] = y
        return 0

    lax.fori_loop(0, NLAT // 4, add_lon, 0)

    arrived(lzx_in.at[pl.ds(0, LATS - 1)], 11)

    @pl.when(solves)
    def _():
        arrived(tx_in.at[pl.ds(0, 7)], 10)

    @pl.when(jnp.logical_not(solves))
    def _():
        arrived(tx_in, 10)

    for h in HALF:
        for k in STATES:
            x = jnp.concatenate([lzx_in[4 * h + g, k] for g in range(4)], axis=0)
            for c in STATES:
                x = x + lon_unit[h][c] * tx_in[2 * k + h, pl.ds(c, 1), :]
            enter[h, k] = x

    sent(segco.at[core], 0)
    sent(pair_out, 1)
    sent(coin.at[pl.ds(1, CHIPS - 1)], 2)
    sent(s_in.at[pl.ds(1, CHIPS - 1)], 3)
    sent(lz_in.at[pl.ds(0, LATS - 1)], 4)
    sent(x_in.at[pl.ds(0, CHIPS - 1)], 5)
    sent(unm.at[other], 6)
    sent(latc.at[pl.ds(0, LATS - 1)], 7)
    sent(lzx_in.at[pl.ds(0, LATS - 1)], 11)

    @pl.when(solves)
    def _():
        sent(sc_in.at[pl.ds(0, 7)], 8)
        sent(t_out.at[pl.ds(0, 7)], 9)
        sent(tx_out.at[pl.ds(1, LONS - 1)], 10)

    @pl.when(jnp.logical_not(solves))
    def _():
        sent(sc_in.at[pl.ds(0, 8)], 8)
        sent(t_out, 9)


def finish(work, latu, enter, std, tw, out, line, out_v, sem):
    parts = 4
    size = ROWS // parts

    for step in range(parts):
        rows = pl.ds(step * size, size)
        for h in HALF:
            for j in range(size // 16):
                i = step * (size // 16) + j
                y = work[h, pl.ds(i * 16, 16), :]
                unit = latu[h, pl.ds(i * 8, 8), :]
                for k in STATES:
                    y = y + unit[k:k + 1] * enter[h, k]
                line[h, pl.ds(16 * j, 16), :] = y
            lanes = pl.ds(h * LANES, LANES)
            out_v[rows, lanes] = std[rows, lanes] * dot3(line[h], tw[h])
        pltpu.make_async_copy(out_v.at[rows], out.at[rows], sem.at[0]).start()

    pltpu.make_async_copy(out_v, out, sem.at[0]).wait()


def per_device(increment, error_std, vertical, lon_decay, lat_decay):
    vmem = lambda *shape: pltpu.VMEM(shape, F32)
    whole = pl.BlockSpec(memory_space=pltpu.VMEM)
    weights = pltpu.VMEM((2, 256, 256), BF16)
    held = pl.pallas_call(
        kernel,
        out_shape=[
            vmem(2, ROWS, LANES), vmem(2, NLAT * 8, LANES), vmem(2, 4, NLON, LANES), vmem(ROWS, 256), weights,
        ],
        in_specs=[pl.BlockSpec(memory_space=pl.ANY)] * 5,
        out_specs=[whole] * 5,
        scratch_shapes=[
            vmem(ROWS, 256), vmem(4, 64, 64), vmem(NLON, 256), vmem(NLAT, 256),
            weights, vmem(2, NLON, 32, LANES), vmem(2, NLON * 8, LANES),
            *[vmem(2, NLAT * 8, LANES)] * 2,
            vmem(2, 4, 32, LANES), vmem(2, 2, 4, 32, LANES), vmem(2, 2, 8, LANES), vmem(2, 8, LANES), vmem(CHIPS, 8, LANES),
            *[vmem(CHIPS, 4, 4, LANES)] * 4,
            vmem(2, 2, 4, 32, LANES), vmem(2, 2, 4, 32, LANES),
            vmem(LATS, 2, 24, LANES), vmem(LATS, 2, 16, LANES), *[vmem(LATS, 4, 4, LANES)] * 4,
            vmem(LONS, 8, LANES), vmem(8, 4, LANES), vmem(LONS, 4, LANES), vmem(LONS, 4, LANES), vmem(8, 4, LANES),
            pltpu.SemaphoreType.DMA((11,)), pltpu.SemaphoreType.DMA((13,)), pltpu.SemaphoreType.DMA((13,)),
        ],
        compiler_params=pltpu.CompilerParams(
            collective_id=0, has_side_effects=True, vmem_limit_bytes=24 * 1024 * 1024
        ),
    )(*[
        pltpu.with_memory_space_constraint(x, pltpu.HBM)
        for x in (increment.reshape(ROWS, 256), error_std.reshape(ROWS, 256), vertical, lon_decay, lat_decay)
    ])
    result = pl.pallas_call(
        finish,
        out_shape=jax.ShapeDtypeStruct((ROWS, 256), F32),
        in_specs=[whole] * 5,
        out_specs=pl.BlockSpec(memory_space=pl.ANY),
        scratch_shapes=[vmem(2, ROWS // 4, LANES), vmem(ROWS, 256), pltpu.SemaphoreType.DMA((1,))],
        compiler_params=pltpu.CompilerParams(vmem_limit_bytes=24 * 1024 * 1024),
    )(*held)
    return result.reshape(NLAT, NLON, 256)


def solution(mesh):
    placed = (P("lat", "lon", None), P("lat", "lon", None), P(), P("lon", None), P("lat", None))
    return jax.shard_map(
        per_device, mesh=mesh, in_specs=placed, out_specs=P("lat", "lon", None), check_vma=False
    )
```

time: 34.5 us -> 33.1 us (0.959)
  Pallas kernels: 34.4 us -> 33 us
    pallas_call x1, Pallas kernels: 32.5 us -> 31.7 us  [per_device(): pl.pallas_call(kernel, out_shape=[vmem(2, ROWS, LANES), vmem(2, NLAT * 8,...]
    pallas_call x1, Pallas kernels: 1.9 us -> 1.31 us  [per_device(): pl.pallas_call(finish, out_shape=jax.ShapeDtypeStruct((ROWS, 256), F32),...]
where the time goes in v3:
time: 33.1 us; the launch traced here: 33 us
  Pallas kernels  33 us (100%)
    pallas_call x1, Pallas kernels, per_device(): pl.pallas_call(kernel, out_shape=[vmem(2, ROWS, LANES), vmem(2, NLAT * 8,...  31.7 us
    pallas_call x1, Pallas kernels, per_device(): pl.pallas_call(finish, out_shape=jax.ShapeDtypeStruct((ROWS, 256), F32),...  1.31 us

profile of v3, /device:TPU:1, one launch (start us, length us, event | category | flops | bytes accessed | tf_op | source)
XLA Modules:
  0.0 33.0 jit_solution(11025481428020955534)
XLA Ops:
  0.0 31.7 %shard_map.55 = (f32[2,1024,128]{2,1,0:T(8,128)S(1)}, f32[2,512,128]{2,1,0:T(8,128)S(1)}, f32[2,4,16,128]{3,2,1,0:T(8,128)S(1)}, f32[1024,256]{1,0:T(8,128)S(1)}, bf16[2,256,256]{2,1,0:T(8,128)(2,1)S(1)}) custom-call(f32[1024,256]{1,0:T(8,128)} %bitcast.3, f32[1024,256]{1,0:T(8,128)} %bitcast.4, f32[4,64,64]{2,1,0:T(8,128)} %vert.1, f32[16,256]{1,0:T(8,128)} %lond.1, ...), custom_call_target="tpu_custom_call" | custom-call | tf_op jit(solution)/shard_map/pallas_call | solution.py:497
  31.7 1.3 %shard_map.56 = f32[1024,256]{1,0:T(8,128)} custom-call(f32[2,1024,128]{2,1,0:T(8,128)S(1)} %get-tuple-element.10.work, f32[2,512,128]{2,1,0:T(8,128)S(1)} %get-tuple-element.11.latu, f32[2,4,16,128]{3,2,1,0:T(8,128)S(1)} %get-tuple-element.12.enter, f32[1024,256]{1,0:T(8,128)S(1)} %get-tuple-element.13.std, bf16[2,256,256]{2,1,0:T(8,128)(2,1)S(1)} %get-tuple-element.14.tw), custom_call_target="tpu_custom_call" | custom-call | tf_op jit(solution)/shard_map/pallas_call | solution.py:522

commit v4 on v3

--- a/solution.py
+++ b/solution.py
@@ -43,7 +43,7 @@
     work, latu, enter, std_v, tw,
     inc_v, vert_v, lond_v, latd_v,
     vw, temp, lonu, adj, xcol,
-    pair_out, seg, segco, chipco, coin,
+    pair_out, seg, segco,
     s_out, s_in, x_out, x_in, unm, xlon,
     latc, latcx, lz_out, lz_in, lzx_out, lzx_in, sc_in, t_out, t_in, tx_out, tx_in,
     lsem, ssem, rsem,
@@ -153,24 +153,12 @@
     lon_sweeps(other, put_out)
     pl.semaphore_wait(barrier, len(greeted))
     send(segco.at[core], segco.at[core], 0, partner)
-
-    solves = lax.rem(lon, 8) // 2 == 1
-    solvers = [(2 * k + h, h, 8 * k + 2 + h) for k in STATES for h in HALF]
-
-    def to_solvers(out, into, which):
-        for n, h, solver in solvers:
-            place = lax.rem(lon - solver + LONS, LONS)
-
-            @pl.when(place != 0)
-            def _():
-                send(out(n, h), into.at[place], which, {"lon": solver})
-
-            @pl.when(place == 0)
-            def _():
-                into[0] = out(n, h)[...]
-
-    to_solvers(lambda n, h: segco.at[core, h], sc_in, 8)
     send(pair_out, seg.at[core], 1, partner)
+
+    lon_half = lambda l: lax.rem(l // 2, 2)
+    for k in FAR_LONS:
+        send(segco.at[core, lon_half(lax.rem(lon + k, LONS))], sc_in.at[LONS - k], 8, lon_peer(k))
+    sc_in[0] = segco[core, lon_half(lon)]
 
     loads[2].wait()
     adj[...] = jnp.zeros_like(adj)
@@ -198,14 +186,15 @@
 
     arrived(segco.at[other], 0)
     co = lambda s, h, r: segco[s, h, pl.ds(r, 1), :]
-    for h in HALF:
-        g_l, a21_l, a32_l, a31_l, a42_l, a41_l = (co(0, h, r) for r in range(6))
-        g_r, a21_r, a32_r, a31_r, a42_r, a41_r = (co(1, h, r) for r in range(6))
+
+    def compose(left, right):
+        g_l, a21_l, a32_l, a31_l, a42_l, a41_l = left
+        g_r, a21_r, a32_r, a31_r, a42_r, a41_r = right
         b1 = a21_r * g_l
         f2 = a32_l * b1 + a31_l
         b2 = a21_r * f2 + a41_r * g_l
         f2b = a32_l * g_r
-        values = (
+        return (
             g_l * g_r,
             g_l * b1 + a21_l,
             g_r * f2b + a32_r,
@@ -213,12 +202,6 @@
             g_l * (a21_r * f2b + a42_r) + a42_l * g_r,
             g_l * b2 + a42_l * b1 + a41_l,
         )
-        for r, value in enumerate(values):
-            chipco[h, pl.ds(r, 1), :] = value
-        chipco[h, pl.ds(6, 2), :] = jnp.zeros((2, LANES), F32)
-    coin[0] = chipco[chip // 8]
-    for k in FAR_CHIPS:
-        send(chipco.at[chip_at(k) // 8], coin.at[CHIPS - k], 2, peer(k))
 
     lon_sweeps(core, put_own)
 
@@ -263,7 +246,7 @@
         merged = merge(h, states(0, h), states(1, h))
         for k in STATES:
             for j in range(8):
-                s_out[8 * h + j, k] = merged[k][4 * j:4 * j + 4]
+                s_out[2 * j + h, k] = merged[k][4 * j:4 * j + 4]
     for k in FAR_CHIPS:
         send(s_out.at[chip_at(k)], s_in.at[CHIPS - k], 3, peer(k))
     s_in[0] = s_out[chip]
@@ -324,14 +307,18 @@
             lambda p, r: latc[p, h, pl.ds(16 + r, 1), :],
             put_c, jnp.zeros((4, LANES), F32),
         )
-    for n, h, _ in solvers:
-        t_out[n] = latcx[lat, h, pl.ds(4 * (n // 2), 4), :]
-    to_solvers(lambda n, h: t_out.at[n], t_in, 9)
+    place = lambda k, h: k % 2 + 2 * h + 4 * (k // 2)
+    for k in STATES:
+        for h in HALF:
+            t_out[place(k, h)] = latcx[lat, h, pl.ds(4 * k, 4), :]
+    for k in FAR_LONS:
+        send(t_out.at[lax.rem(lon + k, 8)], t_in.at[LONS - k], 9, lon_peer(k))
+    t_in[0] = t_out[lax.rem(lon, 8)]
 
     seat = range(CHIPS)
 
-    def ring_maps(seat, row):
-        cc = [[row(j, r) for r in range(6)] for j in seat]
+    def ring_maps(cc):
+        seat = range(len(cc))
         ahead, behind = [jnp.ones((1, LANES), F32)], [jnp.ones((1, LANES), F32)]
         for j in seat:
             ahead.append(ahead[-1] * cc[j][0])
@@ -357,8 +344,10 @@
         x4 = ring([state(j, 3) + cc[j][5] * x1[j] + cc[j][4] * x2[j] + cc[j][1] * x3[j] for j in seat], True)
         return x1, x2, x3, x4
 
-    arrived(coin.at[pl.ds(1, CHIPS - 1)], 2)
-    maps = ring_maps(seat, lambda j, r: coin[j, pl.ds(r, 1), :])
+    arrived(sc_in.at[pl.ds(1, LONS - 1)], 8)
+    rows = lambda j: [sc_in[j, pl.ds(r, 1), :] for r in range(6)]
+    left_at = lambda j: lax.rem(2 * j - core + LONS, LONS)
+    maps = ring_maps([compose(rows(left_at(j)), rows(2 * j + 1 - core)) for j in seat])
     arrived(s_in.at[pl.ds(1, CHIPS - 1)], 3)
     x1, x2, x3, x4 = ring_solve(seat, maps, lambda j, k: s_in[j, k], jnp.zeros((4, LANES), F32))
     for j in seat:
@@ -368,19 +357,17 @@
         send(x_out.at[k], x_in.at[chip], 5, peer(k))
     x_in[chip] = x_out[0]
 
-    @pl.when(solves)
-    def _():
-        devices = range(LONS)
-        arrived(sc_in.at[pl.ds(1, LONS - 1)], 8)
-        maps = ring_maps(devices, lambda j, r: sc_in[j, pl.ds(r, 1), :])
-        arrived(t_in.at[pl.ds(1, LONS - 1)], 9)
-        found = ring_solve(devices, maps, lambda j, c: t_in[j, pl.ds(c, 1), :], jnp.zeros((1, LANES), F32))
-        for j in devices:
-            for c in STATES:
-                tx_out[j, pl.ds(c, 1), :] = found[c][j]
-        for k in FAR_LONS:
-            send(tx_out.at[k], tx_in.at[2 * (lon // 8) + core], 10, lon_peer(k))
-        tx_in[2 * (lon // 8) + core] = tx_out[0]
+    devices = range(LONS)
+    maps = ring_maps([rows(j) for j in devices])
+    arrived(t_in.at[pl.ds(1, LONS - 1)], 9)
+    found = ring_solve(devices, maps, lambda j, c: t_in[j, pl.ds(c, 1), :], jnp.zeros((1, LANES), F32))
+    for j in devices:
+        for c in STATES:
+            tx_out[j, pl.ds(c, 1), :] = found[c][j]
+    for k in range(1, 8):
+        near = 8 * (lon // 8) + lax.rem(lon + k, 8)
+        send(tx_out.at[lax.rem(near - lon + LONS, LONS)], tx_in.at[lax.rem(lon, 8)], 10, {"lon": near})
+    tx_in[lax.rem(lon, 8)] = tx_out[0]
 
     arrived(lz_in.at[pl.ds(0, LATS - 1)], 4)
 
@@ -398,7 +385,7 @@
 
     arrived(x_in.at[pl.ds(0, CHIPS - 1)], 5)
     for h in HALF:
-        entering = [jnp.concatenate([x_in[8 * h + j, k] for j in range(8)], axis=0) for k in STATES]
+        entering = [jnp.concatenate([x_in[2 * j + h, k] for j in range(8)], axis=0) for k in STATES]
         for whose, parts_in in enumerate(unmerge(h, states(0, h), states(1, h), entering)):
             for k in STATES:
                 unm[whose, h, k] = parts_in[k]
@@ -432,24 +419,16 @@
 
     arrived(lzx_in.at[pl.ds(0, LATS - 1)], 11)
 
-    @pl.when(solves)
-    def _():
-        arrived(tx_in.at[pl.ds(0, 7)], 10)
-
-    @pl.when(jnp.logical_not(solves))
-    def _():
-        arrived(tx_in, 10)
-
+    arrived(tx_in.at[pl.ds(0, 7)], 10)
     for h in HALF:
         for k in STATES:
             x = jnp.concatenate([lzx_in[4 * h + g, k] for g in range(4)], axis=0)
             for c in STATES:
-                x = x + lon_unit[h][c] * tx_in[2 * k + h, pl.ds(c, 1), :]
+                x = x + lon_unit[h][c] * tx_in[place(k, h), pl.ds(c, 1), :]
             enter[h, k] = x
 
     sent(segco.at[core], 0)
     sent(pair_out, 1)
-    sent(coin.at[pl.ds(1, CHIPS - 1)], 2)
     sent(s_in.at[pl.ds(1, CHIPS - 1)], 3)
     sent(lz_in.at[pl.ds(0, LATS - 1)], 4)
     sent(x_in.at[pl.ds(0, CHIPS - 1)], 5)
@@ -457,16 +436,9 @@
     sent(latc.at[pl.ds(0, LATS - 1)], 7)
     sent(lzx_in.at[pl.ds(0, LATS - 1)], 11)
 
-    @pl.when(solves)
-    def _():
-        sent(sc_in.at[pl.ds(0, 7)], 8)
-        sent(t_out.at[pl.ds(0, 7)], 9)
-        sent(tx_out.at[pl.ds(1, LONS - 1)], 10)
-
-    @pl.when(jnp.logical_not(solves))
-    def _():
-        sent(sc_in.at[pl.ds(0, 8)], 8)
-        sent(t_out, 9)
+    sent(sc_in.at[pl.ds(1, LONS - 1)], 8)
+    sent(t_in.at[pl.ds(1, LONS - 1)], 9)
+    sent(tx_in.at[pl.ds(0, 7)], 10)
 
 
 def finish(work, latu, enter, std, tw, out, line, out_v, sem):
@@ -505,7 +477,7 @@
             vmem(ROWS, 256), vmem(4, 64, 64), vmem(NLON, 256), vmem(NLAT, 256),
             weights, vmem(2, NLON, 32, LANES), vmem(2, NLON * 8, LANES),
             *[vmem(2, NLAT * 8, LANES)] * 2,
-            vmem(2, 4, 32, LANES), vmem(2, 2, 4, 32, LANES), vmem(2, 2, 8, LANES), vmem(2, 8, LANES), vmem(CHIPS, 8, LANES),
+            vmem(2, 4, 32, LANES), vmem(2, 2, 4, 32, LANES), vmem(2, 2, 8, LANES),
             *[vmem(CHIPS, 4, 4, LANES)] * 4,
             vmem(2, 2, 4, 32, LANES), vmem(2, 2, 4, 32, LANES),
             vmem(LATS, 2, 24, LANES), vmem(LATS, 2, 16, LANES), *[vmem(LATS, 4, 4, LANES)] * 4,

time: 33.1 us -> 31.2 us (0.943)
  Pallas kernels: 33 us -> 31.1 us
    pallas_call x1, Pallas kernels: 31.7 us -> 29.8 us  [per_device(): pl.pallas_call(kernel, out_shape=[vmem(2, ROWS, LANES), vmem(2, NLAT * 8,...]
where the time goes in v4:
time: 31.2 us; the launch traced here: 31.1 us
  Pallas kernels  31.1 us (100%)
    pallas_call x1, Pallas kernels, per_device(): pl.pallas_call(kernel, out_shape=[vmem(2, ROWS, LANES), vmem(2, NLAT * 8,...  29.8 us
    pallas_call x1, Pallas kernels, per_device(): pl.pallas_call(finish, out_shape=jax.ShapeDtypeStruct((ROWS, 256), F32),...  1.31 us

profile of v4, /device:TPU:1, one launch (start us, length us, event | category | flops | bytes accessed | tf_op | source)
XLA Modules:
  0.0 31.1 jit_solution(7796738574014116115)
XLA Ops:
  0.0 29.8 %shard_map.55 = (f32[2,1024,128]{2,1,0:T(8,128)S(1)}, f32[2,512,128]{2,1,0:T(8,128)S(1)}, f32[2,4,16,128]{3,2,1,0:T(8,128)S(1)}, f32[1024,256]{1,0:T(8,128)S(1)}, bf16[2,256,256]{2,1,0:T(8,128)(2,1)S(1)}) custom-call(f32[1024,256]{1,0:T(8,128)} %bitcast.3, f32[1024,256]{1,0:T(8,128)} %bitcast.4, f32[4,64,64]{2,1,0:T(8,128)} %vert.1, f32[16,256]{1,0:T(8,128)} %lond.1, ...), custom_call_target="tpu_custom_call" | custom-call | tf_op jit(solution)/shard_map/pallas_call | solution.py:469
  29.8 1.3 %shard_map.56 = f32[1024,256]{1,0:T(8,128)} custom-call(f32[2,1024,128]{2,1,0:T(8,128)S(1)} %get-tuple-element.10.work, f32[2,512,128]{2,1,0:T(8,128)S(1)} %get-tuple-element.11.latu, f32[2,4,16,128]{3,2,1,0:T(8,128)S(1)} %get-tuple-element.12.enter, f32[1024,256]{1,0:T(8,128)S(1)} %get-tuple-element.13.std, bf16[2,256,256]{2,1,0:T(8,128)(2,1)S(1)} %get-tuple-element.14.tw), custom_call_target="tpu_custom_call" | custom-call | tf_op jit(solution)/shard_map/pallas_call | solution.py:494

commit v5 on v4

--- a/solution.py
+++ b/solution.py
@@ -45,7 +45,7 @@
     vw, temp, lonu, adj, xcol,
     pair_out, seg, segco,
     s_out, s_in, x_out, x_in, unm, xlon,
-    latc, latcx, lz_out, lz_in, lzx_out, lzx_in, sc_in, t_out, t_in, tx_out, tx_in,
+    latc, latco, latcx, lz_out, lz_in, lzx_out, lzx_in, sc_in, t_out, t_in, tx_out, tx_in,
     lsem, ssem, rsem,
 ):
     lon, lat = lax.axis_index("lon"), lax.axis_index("lat")
@@ -155,10 +155,9 @@
     send(segco.at[core], segco.at[core], 0, partner)
     send(pair_out, seg.at[core], 1, partner)
 
-    lon_half = lambda l: lax.rem(l // 2, 2)
-    for k in FAR_LONS:
-        send(segco.at[core, lon_half(lax.rem(lon + k, LONS))], sc_in.at[LONS - k], 8, lon_peer(k))
-    sc_in[0] = segco[core, lon_half(lon)]
+    for k in FAR_CHIPS:
+        send(segco.at[core, lax.rem(chip + k, 2)], sc_in.at[core, CHIPS - k], 8, peer(k))
+    sc_in[core, 0] = segco[core, lax.rem(chip, 2)]
 
     loads[2].wait()
     adj[...] = jnp.zeros_like(adj)
@@ -182,7 +181,9 @@
     carried = [adjoint(k % 2 == 0, [one_hot(k)] * 2) for k in (3, 2, 1, 0)]
     for h in HALF:
         e1, e2 = carried[3][h], carried[2][h]
-        store_coefs(latc, (lat, h), 16, (e1[0:1], e1[1:2], e2[2:3], e1[2:3], e2[3:4], e1[3:4]))
+        store_coefs(latco, (lat, h), 0, (e1[0:1], e1[1:2], e2[2:3], e1[2:3], e2[3:4], e1[3:4]))
+    for k in FAR_LATS:
+        send(latco.at[lat], latco.at[lat], 12, lat_peer(k))
 
     arrived(segco.at[other], 0)
     co = lambda s, h, r: segco[s, h, pl.ds(r, 1), :]
@@ -281,6 +282,9 @@
         send(lz_out.at[lax.rem(lat + k, LATS)], lz_in.at[lat], 4, lat_peer(k))
     lz_in[lat] = lz_out[lat]
 
+    arrived(sc_in.at[core, pl.ds(1, CHIPS - 1)], 8)
+    send(sc_in.at[core], sc_in.at[core], 2, partner)
+
     def lat_solve(state, coef, put, zero):
         x1, x2, x3, x4 = ([zero] * LATS for _ in STATES)
         for p in range(LATS - 1):
@@ -297,6 +301,7 @@
             for k, x in enumerate((x1, x2, x3, x4)):
                 put(p, k, x[p])
 
+    arrived(latco.at[pl.ds(0, LATS - 1)], 12)
     arrived(latc.at[pl.ds(0, LATS - 1)], 7)
     for h in HALF:
         def put_c(p, k, x, h=h):
@@ -304,7 +309,7 @@
 
         lat_solve(
             lambda p, k: latc[p, h, pl.ds(4 * k, 4), :],
-            lambda p, r: latc[p, h, pl.ds(16 + r, 1), :],
+            lambda p, r: latco[p, h, pl.ds(r, 1), :],
             put_c, jnp.zeros((4, LANES), F32),
         )
     place = lambda k, h: k % 2 + 2 * h + 4 * (k // 2)
@@ -344,10 +349,9 @@
         x4 = ring([state(j, 3) + cc[j][5] * x1[j] + cc[j][4] * x2[j] + cc[j][1] * x3[j] for j in seat], True)
         return x1, x2, x3, x4
 
-    arrived(sc_in.at[pl.ds(1, LONS - 1)], 8)
-    rows = lambda j: [sc_in[j, pl.ds(r, 1), :] for r in range(6)]
-    left_at = lambda j: lax.rem(2 * j - core + LONS, LONS)
-    maps = ring_maps([compose(rows(left_at(j)), rows(2 * j + 1 - core)) for j in seat])
+    arrived(sc_in.at[other], 2)
+    rows = lambda c, j: [sc_in[c, j, pl.ds(r, 1), :] for r in range(6)]
+    maps = ring_maps([compose(rows(0, j), rows(1, j)) for j in seat])
     arrived(s_in.at[pl.ds(1, CHIPS - 1)], 3)
     x1, x2, x3, x4 = ring_solve(seat, maps, lambda j, k: s_in[j, k], jnp.zeros((4, LANES), F32))
     for j in seat:
@@ -358,7 +362,7 @@
     x_in[chip] = x_out[0]
 
     devices = range(LONS)
-    maps = ring_maps([rows(j) for j in devices])
+    maps = ring_maps([rows(lax.rem(core + j, 2), lax.rem((core + j) // 2, CHIPS)) for j in devices])
     arrived(t_in.at[pl.ds(1, LONS - 1)], 9)
     found = ring_solve(devices, maps, lambda j, c: t_in[j, pl.ds(c, 1), :], jnp.zeros((1, LANES), F32))
     for j in devices:
@@ -376,7 +380,7 @@
 
     lat_solve(
         lambda p, k: lz_in[p, k],
-        lambda p, r: latc[p, lat // 4, pl.ds(16 + r, 1), :],
+        lambda p, r: latco[p, lat // 4, pl.ds(r, 1), :],
         put_z, jnp.zeros((4, LANES), F32),
     )
     for k in FAR_LATS:
@@ -434,9 +438,11 @@
     sent(x_in.at[pl.ds(0, CHIPS - 1)], 5)
     sent(unm.at[other], 6)
     sent(latc.at[pl.ds(0, LATS - 1)], 7)
+    sent(latco.at[pl.ds(0, LATS - 1)], 12)
     sent(lzx_in.at[pl.ds(0, LATS - 1)], 11)
 
-    sent(sc_in.at[pl.ds(1, LONS - 1)], 8)
+    sent(sc_in.at[core], 2)
+    sent(sc_in.at[core, pl.ds(1, CHIPS - 1)], 8)
     sent(t_in.at[pl.ds(1, LONS - 1)], 9)
     sent(tx_in.at[pl.ds(0, 7)], 10)
 
@@ -480,8 +486,8 @@
             vmem(2, 4, 32, LANES), vmem(2, 2, 4, 32, LANES), vmem(2, 2, 8, LANES),
             *[vmem(CHIPS, 4, 4, LANES)] * 4,
             vmem(2, 2, 4, 32, LANES), vmem(2, 2, 4, 32, LANES),
-            vmem(LATS, 2, 24, LANES), vmem(LATS, 2, 16, LANES), *[vmem(LATS, 4, 4, LANES)] * 4,
-            vmem(LONS, 8, LANES), vmem(8, 4, LANES), vmem(LONS, 4, LANES), vmem(LONS, 4, LANES), vmem(8, 4, LANES),
+            vmem(LATS, 2, 16, LANES), vmem(LATS, 2, 8, LANES), vmem(LATS, 2, 16, LANES), *[vmem(LATS, 4, 4, LANES)] * 4,
+            vmem(2, CHIPS, 8, LANES), vmem(8, 4, LANES), vmem(LONS, 4, LANES), vmem(LONS, 4, LANES), vmem(8, 4, LANES),
             pltpu.SemaphoreType.DMA((11,)), pltpu.SemaphoreType.DMA((13,)), pltpu.SemaphoreType.DMA((13,)),
         ],
         compiler_params=pltpu.CompilerParams(

time: 31.2 us -> 30.1 us (0.965)
  Pallas kernels: 31.1 us -> 30 us
    pallas_call x1, Pallas kernels: 29.8 us -> 28.7 us  [per_device(): pl.pallas_call(kernel, out_shape=[vmem(2, ROWS, LANES), vmem(2, NLAT * 8,...]
where the time goes in v5:
time: 30.1 us; the launch traced here: 30 us
  Pallas kernels  30 us (100%)
    pallas_call x1, Pallas kernels, per_device(): pl.pallas_call(kernel, out_shape=[vmem(2, ROWS, LANES), vmem(2, NLAT * 8,...  28.7 us
    pallas_call x1, Pallas kernels, per_device(): pl.pallas_call(finish, out_shape=jax.ShapeDtypeStruct((ROWS, 256), F32),...  1.31 us

profile of v5, /device:TPU:1, one launch (start us, length us, event | category | flops | bytes accessed | tf_op | source)
XLA Modules:
  0.0 30.0 jit_solution(18135710332594843800)
XLA Ops:
  0.0 28.7 %shard_map.55 = (f32[2,1024,128]{2,1,0:T(8,128)S(1)}, f32[2,512,128]{2,1,0:T(8,128)S(1)}, f32[2,4,16,128]{3,2,1,0:T(8,128)S(1)}, f32[1024,256]{1,0:T(8,128)S(1)}, bf16[2,256,256]{2,1,0:T(8,128)(2,1)S(1)}) custom-call(f32[1024,256]{1,0:T(8,128)} %bitcast.3, f32[1024,256]{1,0:T(8,128)} %bitcast.4, f32[4,64,64]{2,1,0:T(8,128)} %vert.1, f32[16,256]{1,0:T(8,128)} %lond.1, ...), custom_call_target="tpu_custom_call" | custom-call | tf_op jit(solution)/shard_map/pallas_call | solution.py:475
  28.7 1.3 %shard_map.56 = f32[1024,256]{1,0:T(8,128)} custom-call(f32[2,1024,128]{2,1,0:T(8,128)S(1)} %get-tuple-element.10.work, f32[2,512,128]{2,1,0:T(8,128)S(1)} %get-tuple-element.11.latu, f32[2,4,16,128]{3,2,1,0:T(8,128)S(1)} %get-tuple-element.12.enter, f32[1024,256]{1,0:T(8,128)S(1)} %get-tuple-element.13.std, bf16[2,256,256]{2,1,0:T(8,128)(2,1)S(1)} %get-tuple-element.14.tw), custom_call_target="tpu_custom_call" | custom-call | tf_op jit(solution)/shard_map/pallas_call | solution.py:500

commit v6 on v5

--- a/solution.py
+++ b/solution.py
@@ -152,8 +152,8 @@
 
     lon_sweeps(other, put_out)
     pl.semaphore_wait(barrier, len(greeted))
+    send(pair_out, seg.at[core], 1, partner)
     send(segco.at[core], segco.at[core], 0, partner)
-    send(pair_out, seg.at[core], 1, partner)
 
     for k in FAR_CHIPS:
         send(segco.at[core, lax.rem(chip + k, 2)], sc_in.at[core, CHIPS - k], 8, peer(k))
@@ -448,7 +448,7 @@
 
 
 def finish(work, latu, enter, std, tw, out, line, out_v, sem):
-    parts = 4
+    parts = 8
     size = ROWS // parts
 
     for step in range(parts):
@@ -502,7 +502,7 @@
         out_shape=jax.ShapeDtypeStruct((ROWS, 256), F32),
         in_specs=[whole] * 5,
         out_specs=pl.BlockSpec(memory_space=pl.ANY),
-        scratch_shapes=[vmem(2, ROWS // 4, LANES), vmem(ROWS, 256), pltpu.SemaphoreType.DMA((1,))],
+        scratch_shapes=[vmem(2, ROWS // 8, LANES), vmem(ROWS, 256), pltpu.SemaphoreType.DMA((1,))],
         compiler_params=pltpu.CompilerParams(vmem_limit_bytes=24 * 1024 * 1024),
     )(*held)
     return result.reshape(NLAT, NLON, 256)

time: 30.1 us -> 30.1 us (level)
  no operation moved by 1% of the time
where the time goes in v6:
time: 30.1 us; the launch traced here: 29.9 us
  Pallas kernels  29.9 us (99%)
    pallas_call x1, Pallas kernels, per_device(): pl.pallas_call(kernel, out_shape=[vmem(2, ROWS, LANES), vmem(2, NLAT * 8,...  28.6 us
    pallas_call x1, Pallas kernels, per_device(): pl.pallas_call(finish, out_shape=jax.ShapeDtypeStruct((ROWS, 256), F32),...  1.28 us

profile of v6, /device:TPU:1, one launch (start us, length us, event | category | flops | bytes accessed | tf_op | source)
XLA Modules:
  0.0 29.9 jit_solution(11485232505914899586)
XLA Ops:
  0.0 28.6 %shard_map.55 = (f32[2,1024,128]{2,1,0:T(8,128)S(1)}, f32[2,512,128]{2,1,0:T(8,128)S(1)}, f32[2,4,16,128]{3,2,1,0:T(8,128)S(1)}, f32[1024,256]{1,0:T(8,128)S(1)}, bf16[2,256,256]{2,1,0:T(8,128)(2,1)S(1)}) custom-call(f32[1024,256]{1,0:T(8,128)} %bitcast.3, f32[1024,256]{1,0:T(8,128)} %bitcast.4, f32[4,64,64]{2,1,0:T(8,128)} %vert.1, f32[16,256]{1,0:T(8,128)} %lond.1, ...), custom_call_target="tpu_custom_call" | custom-call | tf_op jit(solution)/shard_map/pallas_call | solution.py:475
  28.7 1.3 %shard_map.56 = f32[1024,256]{1,0:T(8,128)} custom-call(f32[2,1024,128]{2,1,0:T(8,128)S(1)} %get-tuple-element.10.work, f32[2,512,128]{2,1,0:T(8,128)S(1)} %get-tuple-element.11.latu, f32[2,4,16,128]{3,2,1,0:T(8,128)S(1)} %get-tuple-element.12.enter, f32[1024,256]{1,0:T(8,128)S(1)} %get-tuple-element.13.std, bf16[2,256,256]{2,1,0:T(8,128)(2,1)S(1)} %get-tuple-element.14.tw), custom_call_target="tpu_custom_call" | custom-call | tf_op jit(solution)/shard_map/pallas_call | solution.py:500
